TPU v7x, 128 devices: a whole 4x4x4 slice. The times are simulated.
128 devices in a mesh: blk: 8 (over y_lo, x), head: 16 (over y_hi, z, core).
Axes of the slice: x: 4, y: 4 (y_hi: 2, y_lo: 2; y = y_hi * 2 + y_lo), z: 4, core: 2. Of those that a mesh axis runs over, the one named last changes fastest.
Arguments:
- q_vals: bfloat16 [8192, 6144], P(('blk', 'head')), may hold values from -96 to 96
- k_vals: bfloat16 [8192, 6144], P(('blk', 'head')), may hold values from -8 to 8
- v_vals: bfloat16 [8192, 6144], P(('blk', 'head')), may hold values from -6 to 6
- q_scale: bfloat16 [8192, 48], P(('blk', 'head')), may hold values from 0.4 to 2.5
- k_scale: bfloat16 [8192, 48], P(('blk', 'head')), may hold values from 0.4 to 2.5
- v_scale: bfloat16 [8192, 48], P(('blk', 'head')), may hold values from 0.3984375 to 2.5
- out_weight: bfloat16 [6144, 6144], P('head'), may hold values from -0.109375 to 0.109375
Outputs:
- targets: bfloat16 [8192, 6144], P('blk', 'head')
All inputs are finite; a program needn't handle non-finite values.
Results may differ from a plain program's by a relative error of at most 0.023.
Values may be sent and summed in bfloat16 or wider, within the bound.
No kernel may reach another device: no remote copies, remote signals or barrier semaphores. Data moves between devices by JAX's collectives and lax.ppermute only.
A program may use at most 128 MiB of HBM per device.

v0:
```python
import functools

import jax
import jax.numpy as jnp
from jax import lax
from jax.experimental import pallas as pl
from jax.experimental.pallas import tpu as pltpu
from jax.sharding import Mesh, PartitionSpec as P

AXES = ("ylo", "x", "yhi", "z", "core")
HSIZE = 128
HPG = 3
GROUPS = 16
BLOCK = 512
STATS = 16
FACTOR = 1.4426950408889634 / HSIZE**0.5
SCALE = 1.6
BF = jnp.bfloat16
F32 = jnp.float32
ANY = pl.BlockSpec(memory_space=pl.ANY)


def params(mib):
    return pltpu.CompilerParams(vmem_limit_bytes=mib * 2**20)


def cost(us):
    return pl.CostEstimate(flops=int(us * SCALE * 1.15e9), bytes_accessed=10**5, transcendentals=0)


def gate(a, *tokens):
    return pl.pallas_call(
        lambda *refs: None,
        in_specs=[ANY] * (1 + len(tokens)),
        out_specs=ANY,
        out_shape=jax.ShapeDtypeStruct(a.shape, a.dtype),
        input_output_aliases={0: 0},
        cost_estimate=cost(0.01),
    )(a, *tokens)


def group_of(dest):
    ylo, yhi, z = dest // 8, (dest // 4) % 2, dest % 4
    return yhi * 8 + z * 2 + ylo


def dequant_kernel(q_ref, k_ref, v_ref, qs_ref, ks_ref, vs_ref, *refs, heads):
    o_ref = refs[-1]
    scales = [r[...].astype(F32).T for r in (qs_ref, ks_ref, vs_ref)]
    scales[0] = scales[0] * FACTOR
    for dest in range(GROUPS):
        for i, head in enumerate(heads):
            col = group_of(dest) * HPG + head
            for part, ref in enumerate((q_ref, k_ref, v_ref)):
                at = i if part == 0 else len(heads) + 2 * i + part - 1
                vals = ref[:, col * HSIZE : (col + 1) * HSIZE].astype(F32)
                o_ref[dest, :, at * HSIZE : (at + 1) * HSIZE] = (
                    vals * scales[part][:, col : col + 1]
                ).astype(BF)


def dequant(heads, args, *tokens):
    tok = args[0].shape[0]
    return pl.pallas_call(
        functools.partial(dequant_kernel, heads=heads),
        in_specs=[pl.BlockSpec(memory_space=pltpu.VMEM)] * len(args) + [ANY] * len(tokens),
        out_shape=jax.ShapeDtypeStruct((GROUPS, tok, 3 * len(heads) * HSIZE), BF),
        compiler_params=params(56),
        cost_estimate=cost(3),
    )(*args, *tokens)


def attend_kernel(at_ref, *refs, pieces, queries, tokens):
    q_refs, refs = refs[:queries], refs[queries:]
    kv, refs = refs[: len(pieces)], refs[len(pieces) + tokens :]
    o_refs, vaug = refs[:-1], refs[-1]
    step = pl.program_id(0)

    @pl.when(step == 0)
    def _():
        vaug[:, HSIZE:] = jnp.ones((vaug.shape[0], HSIZE), BF)
        low = 0
        for ref, size in zip(kv, pieces):
            vaug[low : low + size, :HSIZE] = ref[:, HSIZE:]
            low += size

    query = q_refs[0][...]
    if queries > 1:
        query = jnp.where(step < 2, query, q_refs[1][...])

    def score(j):
        return lax.dot_general(
            query, kv[j][:, :HSIZE], (((1,), (1,)), ((), ())), preferred_element_type=F32
        )

    peak = accum = None
    now = score(0)
    low = 0
    for j, size in enumerate(pieces):
        later = score(j + 1) if j + 1 < len(pieces) else None
        top = jnp.max(now, axis=1, keepdims=True)
        newpeak = top if peak is None else jnp.maximum(peak, top)
        weight = jnp.exp2((now - newpeak).astype(BF))
        term = jnp.dot(weight, vaug[low : low + size, :], preferred_element_type=F32)
        accum = term if accum is None else accum * jnp.exp2(peak - newpeak) + term
        peak, now, low = newpeak, later, low + size
    total = accum[:, HSIZE:]
    out = (accum[:, :HSIZE] / total).astype(BF)
    logsum = peak + jnp.log2(total)
    line = logsum.T[:1, :]
    line = jnp.concatenate(
        [line[:, r * HSIZE : (r + 1) * HSIZE] for r in range(BLOCK // HSIZE)], axis=0
    )
    first = line.astype(BF).astype(F32)
    second = (line - first).astype(BF).astype(F32)
    third = line - first - second
    rows = jnp.concatenate([first, second, third, jnp.zeros_like(line)], axis=0).astype(BF)
    for i, o_ref in enumerate(o_refs):

        @pl.when(step // 2 == i)
        def _():
            o_ref[0, :BLOCK, :] = out
            o_ref[0, BLOCK:, :] = rows


def attend(ylo, queries, kv, tokens=()):
    n = len(queries)
    pieces = tuple(a.shape[0] for a, _ in kv)

    def query(i, col):
        return pl.BlockSpec(
            (BLOCK, HSIZE), lambda g, s: (((g if n == 1 else jnp.clip(g - 2 * i, 0, 1)) + s[0]) % 2, col)
        )

    def piece(a, col):
        return pl.BlockSpec((a.shape[0], 2 * HSIZE), lambda g, s: (0, col))

    def result(i):
        return pl.BlockSpec(
            (1, BLOCK + STATS, HSIZE), lambda g, s: (jnp.clip(g - 2 * i, 0, 1), 0, 0)
        )

    return pl.pallas_call(
        functools.partial(attend_kernel, pieces=pieces, queries=n, tokens=len(tokens)),
        grid_spec=pltpu.PrefetchScalarGridSpec(
            num_scalar_prefetch=1,
            grid=(2 * n,),
            in_specs=[
                *[query(i, col) for i, (_, col) in enumerate(queries)],
                *[piece(*a) for a in kv],
                *[ANY] * len(tokens),
            ],
            out_specs=[result(i) for i in range(n)],
            scratch_shapes=[pltpu.VMEM((sum(pieces), 2 * HSIZE), BF)],
        ),
        out_shape=[jax.ShapeDtypeStruct((2, BLOCK + STATS, HSIZE), BF)] * n,
        compiler_params=params(30),
        cost_estimate=cost(6.5 * n),
    )(ylo, *[a for a, _ in queries], *[a for a, _ in kv], *tokens)


def combine_kernel(a, b, *refs):
    outs = refs[-2:]

    def logsum(ref, half):
        s = ref[half, BLOCK:, :].astype(F32)
        s = s[:4] + s[4:8] + s[8:12]
        return jnp.concatenate(
            [jnp.broadcast_to(s[r : r + 1], (HSIZE, HSIZE)).T for r in range(4)], axis=0
        )

    for half in range(2):
        la, lb = logsum(a, half), logsum(b, half)
        top = jnp.maximum(la, lb)
        wa, wb = jnp.exp2(la - top), jnp.exp2(lb - top)
        out = a[half, :BLOCK, :].astype(F32) * wa + b[half, :BLOCK, :].astype(F32) * wb
        outs[half][...] = (out / (wa + wb)).astype(BF)


def combine(a, b, *tokens):
    vmem = pl.BlockSpec(memory_space=pltpu.VMEM)
    return pl.pallas_call(
        combine_kernel,
        in_specs=[vmem] * 2 + [ANY] * len(tokens),
        out_shape=[jax.ShapeDtypeStruct((BLOCK, HSIZE), BF)] * 2,
        compiler_params=params(12),
        cost_estimate=cost(2),
    )(a, b, *tokens)


def ring(n, step):
    return [(i, (i + step) % n) for i in range(n)]


def opposite_y(a, flip=False):
    perm = []
    for yhi in range(2):
        for core in range(2):
            perm.append((yhi * 2 + core, (1 - yhi) * 2 + (1 - core if flip else core)))
    return lax.ppermute(a, ("yhi", "core"), perm)


def swap(a):
    return lax.ppermute(a, "core", [(0, 1), (1, 0)])


def other_ylo(a):
    return lax.ppermute(a, "ylo", [(0, 1), (1, 0)])


def key_pair(a):
    return lax.ppermute(a, "x", [(0, 1), (1, 0), (2, 3), (3, 2)])


def query_pair(a):
    return lax.ppermute(a, "x", [(0, 3), (3, 0), (1, 2), (2, 1)])


def ring_gather(to_next, to_last, to_far):
    return [
        lax.ppermute(to_next, "z", ring(4, 1)),
        lax.ppermute(to_last, "z", ring(4, -1)),
        lax.ppermute(to_far, "z", ring(4, 2)),
    ]


def pack_kernel(w_ref, token_ref, o_ref):
    half = w_ref.shape[1] // 2
    width = half // 4
    for to in range(4):
        for yhi in range(2):
            low = yhi * half + to * width
            o_ref[to, :, yhi * width : (yhi + 1) * width] = w_ref[:, low : low + width]


def pack_weight(out_weight, token):
    rows, width = out_weight.shape
    return pl.pallas_call(
        pack_kernel,
        in_specs=[pl.BlockSpec(memory_space=pltpu.VMEM), ANY],
        out_shape=jax.ShapeDtypeStruct((4, rows, width // 4), BF),
        compiler_params=params(56),
        cost_estimate=cost(4),
    )(out_weight, token)


def project_kernel(at_ref, *refs, head, before, last, tokens):
    blocks, w, refs = refs[:4], refs[4:6], refs[6:]
    start, refs = refs[:before], refs[before + tokens :]
    outs, (left, right, sems) = refs[: 4 if last else 1], refs[4 if last else 1 :]
    cols = right.shape[1] // 4
    core, apart, yhi, z = at_ref[0], at_ref[1], at_ref[2], at_ref[3]
    copies = []
    for i, off in enumerate((0, 3, 1, 2) * 2):
        group = w[i // 4].at[lax.rem(z + off, 4)]
        for j in range(4):
            low = (lax.rem(yhi + 1 + j // 2, 2) * 2 + lax.rem(core + j, 2)) * cols
            copies.append(
                pltpu.make_async_copy(
                    group.at[pl.ds(head * HSIZE, HSIZE), pl.ds(pl.multiple_of(low, cols), cols)],
                    right.at[pl.ds(i * HSIZE, HSIZE), pl.ds(j * cols, cols)],
                    sems.at[len(copies)],
                )
            )
    for copy in copies:
        copy.start()
    for p in range(2):
        low = pl.multiple_of(lax.rem(apart + p, 2) * HSIZE, HSIZE)
        for r in range(4):
            at = (p * 4 + r) * HSIZE
            left[:, at : at + HSIZE] = blocks[r][:, pl.ds(low, HSIZE)]
    for copy in copies:
        copy.wait()
    out = jnp.dot(left[...], right[...], preferred_element_type=F32)
    if before:
        out = out + start[0][...]
    if last:
        for j in range(4):
            outs[j][...] = out[:, j * cols : (j + 1) * cols].astype(BF)
    else:
        outs[0][...] = out


def project(at, head, blocks, weights, before=(), last=False, tokens=()):
    cols = weights[0].shape[1]
    vmem = pl.BlockSpec(memory_space=pltpu.VMEM)
    if last:
        out_shape = [jax.ShapeDtypeStruct((BLOCK, cols), BF)] * 4
    else:
        out_shape = jax.ShapeDtypeStruct((BLOCK, 4 * cols), F32)
    return pl.pallas_call(
        functools.partial(
            project_kernel, head=head, before=len(before), last=last, tokens=len(tokens)
        ),
        in_specs=[pl.BlockSpec(memory_space=pltpu.SMEM)]
        + [vmem] * 4
        + [ANY] * 2
        + [vmem] * len(before)
        + [ANY] * len(tokens),
        out_shape=out_shape,
        scratch_shapes=[
            pltpu.VMEM((BLOCK, 8 * HSIZE), BF),
            pltpu.VMEM((8 * HSIZE, 4 * cols), BF),
            pltpu.SemaphoreType.DMA((32,)),
        ],
        compiler_params=params(20),
        cost_estimate=cost(3),
    )(at, *blocks, *weights, *before, *tokens)


def on_device(q_vals, k_vals, v_vals, q_scale, k_scale, v_scale, out_weight):
    cols = out_weight.shape[0]
    tok = q_vals.shape[0]
    ylo, yhi, z, core = (lax.axis_index(n) for n in ("ylo", "yhi", "z", "core"))
    mine = ylo.reshape(1)
    every = ("ylo", "yhi", "z")

    def exchange(a):
        a = lax.all_to_all(a, every, split_axis=0, concat_axis=0, tiled=True)
        return a.reshape(-1, a.shape[2])

    parts = (q_vals, k_vals, v_vals, q_scale.T, k_scale.T, v_scale.T)
    d1 = dequant((0, 1), parts)
    d2 = dequant((2,), parts, d1)
    packed = pack_weight(out_weight, d1)
    e1 = gate(exchange(d1), d2, packed)
    q1, kv0, kv1 = (e1[:, i * 2 * HSIZE : (i + 1) * 2 * HSIZE] for i in range(3))
    near0 = key_pair(kv0)
    theirs1 = query_pair(q1)
    s1 = swap(e1)
    e2 = exchange(gate(d2, e1))
    near1 = key_pair(gate(kv1, near0))
    snear0 = swap(near0)
    q2, kv2 = e2[:, :HSIZE], e2[:, HSIZE:]
    theirs2 = query_pair(q2)
    near2 = key_pair(gate(kv2, near1))
    s2 = swap(kv2)
    snear1, snear2 = swap(near1), swap(near2)
    moved = lax.all_to_all(gate(packed, e2), "z", split_axis=0, concat_axis=0, tiled=True)

    keys0 = [(e1, 1), (s1, 1), (near0, 0), (snear0, 0)]
    keys1 = [(e1, 2), (s1, 2), (near1, 0), (snear1, 0)]
    keys2 = [(kv2, 0), (s2, 0), (near2, 0), (snear2, 0)]

    def widen(keep, send):
        return jnp.concatenate([keep, other_ylo(send)], axis=1)

    def gather(both):
        return [both, *ring_gather(both, both, both)]

    (kept0,) = attend(mine, [(e1, 0)], keys0)
    (sent0,) = attend(mine, [(theirs1, 0)], keys0, (kept0,))
    back0 = query_pair(sent0)
    (sent1,) = attend(mine, [(theirs1, 1)], keys1, (sent0,))
    back1 = query_pair(sent1)
    rows0 = combine(kept0, back0, sent1)
    (kept1,) = attend(mine, [(e1, 1)], keys1, (rows0[0],))
    both0 = widen(*rows0)
    rows1 = combine(kept1, back1)
    (sent2,) = attend(mine, [(theirs2, 0)], keys2, (rows1[0], both0))
    set0 = gather(both0)
    back2 = query_pair(sent2)
    both1 = widen(*rows1)
    (kept2,) = attend(mine, [(q2, 0)], keys2, (sent2, both1))
    set1 = gather(both1)
    rows2 = combine(kept2, back2, *set0[1:])
    moved = gate(moved, rows2[0])
    weights = [moved, swap(moved)]
    both2 = widen(*rows2)
    set2 = gather(both2)
    at = jnp.stack([core, jnp.where(core == ylo, 0, 1), yhi, z])
    out = project(at, 0, set0, weights, tokens=(both2, *set1[1:]))
    out = project(at, 1, set1, weights, (out,))
    out = project(at, 2, set2, weights, (out,), last=True)
    own = out[2].astype(F32) + opposite_y(out[0]).astype(F32)
    other = swap(out[3]).astype(F32) + opposite_y(out[1], flip=True).astype(F32)
    own, other = own.astype(BF), other.astype(BF)
    one = jnp.where(core == 0, own, other).reshape(-1, tok, cols)
    two = jnp.where(core == 0, other, own).reshape(-1, tok, cols)
    return jnp.stack([one, two], axis=1).reshape(-1, cols)


def solution(mesh):
    fine = Mesh(mesh.devices.reshape(2, 4, 2, 4, 2), AXES)
    return jax.shard_map(
        on_device,
        mesh=fine,
        in_specs=(P(AXES, None),) * 6 + (P(("yhi", "z", "core"), None),),
        out_specs=P(("ylo", "x"), ("yhi", "z", "core")),
        check_vma=False,
    )
```

profile of v0, /device:TPU:1, one launch (start us, length us, event | category | flops | bytes accessed | tf_op | source)
XLA Modules:
  0.0 184.9 jit_solution(11672742091388255332)
XLA Ops:
  0.0 3.5 %shard_map.73.refs_0_.token_ref = bf16[16,64,768]{2,1,0:T(8,128)(2,1)} custom-call(bf16[64,6144]{1,0:T(8,128)(2,1)} %q_ref.3, bf16[64,6144]{1,0:T(8,128)(2,1)} %k_ref.3, bf16[64,6144]{1,0:T(8,128)(2,1)} %v_ref.3, bf16[48,64]{1,0:T(8,128)(2,1)} %bitcast.19, bf16[48,64]{1,0:T(8,128)(2,1)} %bitcast.21, bf16[48,64]{1,0:T(8,128)(2,1)} %bitcast.23), custom_call_target="tpu_custom_call" | custom-call | flops 5520000000 | bytes 100000 | tf_op jit(solution)/shard_map/pallas_call | solution.py:64
  3.5 8.6 %all-to-all-start = ((bf16[16,64,768]{2,1,0:T(8,128)(2,1)}), bf16[16,64,768]{2,1,0:T(8,128)(2,1)S(1)}, u32[]{:S(2)}, u32[]{:S(2)}) async-start(bf16[16,64,768]{2,1,0:T(8,128)(2,1)} %shard_map.73.refs_0_.token_ref), calls=%async_computation | async-start | bytes 3145728 | tf_op jit(solution)/shard_map/all_to_all | solution.py:319
  12.1 3.0 %shard_map.74.refs_1_.refs_0_ = bf16[16,64,384]{2,1,0:T(8,128)(2,1)} custom-call(bf16[64,6144]{1,0:T(8,128)(2,1)} %q_ref.3, bf16[64,6144]{1,0:T(8,128)(2,1)} %k_ref.3, bf16[64,6144]{1,0:T(8,128)(2,1)} %v_ref.3, bf16[48,64]{1,0:T(8,128)(2,1)} %bitcast.20, bf16[48,64]{1,0:T(8,128)(2,1)} %bitcast.22, bf16[48,64]{1,0:T(8,128)(2,1)} %bitcast.24, ...), custom_call_target="tpu_custom_call" | custom-call | flops 5520000000 | bytes 100000 | tf_op jit(solution)/shard_map/pallas_call | solution.py:64
  15.1 4.8 %shard_map.75.refs_2_.refs_0_ = bf16[4,384,1536]{2,1,0:T(8,128)(2,1)} custom-call(bf16[384,6144]{1,0:T(8,128)(2,1)} %w_ref.1, bf16[16,64,768]{2,1,0:T(8,128)(2,1)} %shard_map.73.refs_0_.token_ref), custom_call_target="tpu_custom_call" | custom-call | flops 7360000000 | bytes 100000 | tf_op jit(solution)/shard_map/pallas_call | solution.py:238
  19.9 12.5 %all-to-all-done = bf16[16,64,768]{2,1,0:T(8,128)(2,1)S(1)} async-done(((bf16[16,64,768]{2,1,0:T(8,128)(2,1)}), bf16[16,64,768]{2,1,0:T(8,128)(2,1)S(1)}, u32[]{:S(2)}, u32[]{:S(2)}) %all-to-all-start) | async-done | bytes 1572896 | tf_op jit(solution)/shard_map/all_to_all | solution.py:319
  33.6 2.5 %collective-permute-start.6 = (bf16[1024,768]{1,0:T(8,128)(2,1)}, bf16[1024,768]{1,0:T(8,128)(2,1)}, u32[]{:S(2)}, u32[]{:S(2)}) collective-permute-start(bf16[1024,768]{1,0:T(8,128)(2,1)} %shard_map.76.refs_1_.refs_0_), channel_id=1, source_target_pairs={{0,1},{1,0},{2,3},{3,2},{4,5},{5,4},{6,7},{7,6},{8,9},{9,8},{10,11... | collective-permute-start | bytes 4718600 | tf_op jit(solution)/shard_map/ppermute | solution.py:204
  36.1 2.5 %fusion = (bf16[1024,256]{1,0:T(8,128)(2,1)}, bf16[1024,256]{1,0:T(8,128)(2,1)S(1)}, bf16[1024,256]{1,0:T(8,128)(2,1)}) fusion(bf16[1024,768]{1,0:T(8,128)(2,1)} %shard_map.76.refs_1_.refs_0_), kind=kLoop, calls=%fused_computation.12 | loop fusion | bytes 3145728 | tf_op jit(solution)/shard_map/slice | solution.py:327
  39.8 4.4 %all-to-all-start.1 = ((bf16[16,64,384]{2,1,0:T(8,128)(2,1)}), bf16[16,64,384]{2,1,0:T(8,128)(2,1)S(1)}, u32[]{:S(2)}, u32[]{:S(2)}) async-start(bf16[16,64,384]{2,1,0:T(8,128)(2,1)} %shard_map.77), calls=%async_computation.1 | async-start | bytes 1572864 | tf_op jit(solution)/shard_map/all_to_all | solution.py:319
  44.2 7.9 %collective-permute-done.1.refs_1_.refs_3_ = bf16[1024,256]{1,0:T(8,128)(2,1)S(1)} collective-permute-done((bf16[1024,256]{1,0:T(8,128)(2,1)S(1)}, bf16[1024,256]{1,0:T(8,128)(2,1)S(1)}, u32[]{:S(2)}, u32[]{:S(2)}) %collective-permute-start.1) | collective-permute-done | bytes 524320 | tf_op jit(solution)/shard_map/ppermute | solution.py:212
  55.2 1.8 collective-permute-start.9
  58.0 1.9 %collective-permute-start = (bf16[1024,256]{1,0:T(8,128)(2,1)S(1)}, bf16[1024,256]{1,0:T(8,128)(2,1)}, u32[]{:S(2)}, u32[]{:S(2)}) collective-permute-start(bf16[1024,256]{1,0:T(8,128)(2,1)S(1)} %slice.21.refs_1_), channel_id=1, source_target_pairs={{0,1},{1,0},{2,3},{3,2},{4,5},{5,4},{6,7},{7,6},{8,9},{9,8},{10,11... | collective-permute-start | bytes 1572872 | tf_op jit(solution)/shard_map/ppermute | solution.py:204
  60.0 5.1 %all-to-all-start.2 = ((bf16[4,384,1536]{2,1,0:T(8,128)(2,1)}), bf16[4,384,1536]{2,1,0:T(8,128)(2,1)}, u32[]{:S(2)}, u32[]{:S(2)}) async-start(bf16[4,384,1536]{2,1,0:T(8,128)(2,1)} %shard_map.89), calls=%async_computation.2 | async-start | bytes 9437184 | tf_op jit(solution)/shard_map/all_to_all | solution.py:339
  65.9 2.5 %collective-permute-start.5 = (bf16[1024,128]{1,0:T(8,128)(2,1)S(1)}, bf16[1024,128]{1,0:T(8,128)(2,1)}, u32[]{:S(2)}, u32[]{:S(2)}) collective-permute-start(bf16[1024,128]{1,0:T(8,128)(2,1)S(1)} %slice.20.refs_0_), channel_id=1, source_target_pairs={{0,48},{48,0},{16,32},{32,16},{1,49},{49,1},{17,33},{33,17},{2,50}... | collective-permute-start | bytes 786440 | tf_op jit(solution)/shard_map/ppermute | solution.py:216
  68.4 2.1 %collective-permute-start.7 = (bf16[1024,256]{1,0:T(8,128)(2,1)}, bf16[1024,256]{1,0:T(8,128)(2,1)S(1)}, u32[]{:S(2)}, u32[]{:S(2)}) collective-permute-start(bf16[1024,256]{1,0:T(8,128)(2,1)} %copy-done.4), channel_id=1, source_target_pairs={{0,1},{1,0},{2,3},{3,2},{4,5},{5,4},{6,7},{7,6},{8,9},{9,8},{10,11... | collective-permute-start | bytes 1572872 | tf_op jit(solution)/shard_map/ppermute | solution.py:204
  70.5 7.0 %shard_map.80.refs_5_.a = bf16[2,528,128]{2,1,0:T(8,128)(2,1)S(1)} custom-call(s32[1]{0:T(128)} %bitcast.4.at_ref, bf16[1024,768]{1,0:T(8,128)(2,1)S(1)} %copy-done.1, bf16[1024,768]{1,0:T(8,128)(2,1)S(1)} %copy-done.1, bf16[1024,768]{1,0:T(8,128)(2,1)} %collective-permute-done.6.refs_2_, bf16[1024,256]{1,0:T(8,128)(2,1)S(1)} %copy-done.7, ...), custom_call_target="tpu_custom_call" | custom-call | flops 11960000512 | bytes 100000 | tf_op jit(solution)/shard_map/pallas_call | solution.py:143
  77.5 7.1 %shard_map.81.refs_5_ = bf16[2,528,128]{2,1,0:T(8,128)(2,1)S(1)} custom-call(s32[1]{0:T(128)} %bitcast.4.at_ref, bf16[1024,256]{1,0:T(8,128)(2,1)} %collective-permute-done.9.refs_0_, bf16[1024,768]{1,0:T(8,128)(2,1)S(1)} %copy-done.1, bf16[1024,768]{1,0:T(8,128)(2,1)} %collective-permute-done.6.refs_2_, bf16[1024,256]{1,0:T(8,128)(2,1)S(1)} %copy-done.7, ...), custom_call_target="tpu_custom_call" | custom-call | flops 11960000512 | bytes 100000 | tf_op jit(solution)/shard_map/pallas_call | solution.py:143
  86.0 6.8 %shard_map.82.refs_0_ = bf16[2,528,128]{2,1,0:T(8,128)(2,1)S(1)} custom-call(s32[1]{0:T(128)} %bitcast.4.at_ref, bf16[1024,256]{1,0:T(8,128)(2,1)} %collective-permute-done.9.refs_0_, bf16[1024,768]{1,0:T(8,128)(2,1)S(1)} %copy-done.1, bf16[1024,768]{1,0:T(8,128)(2,1)} %collective-permute-done.6.refs_2_, bf16[1024,256]{1,0:T(8,128)(2,1)S(1)} %copy-done.5, ...), custom_call_target="tpu_custom_call" | custom-call | flops 11960000512 | bytes 100000 | tf_op jit(solution)/shard_map/pallas_call | solution.py:143
  95.9 6.8 %shard_map.84.a = bf16[2,528,128]{2,1,0:T(8,128)(2,1)S(1)} custom-call(s32[1]{0:T(128)} %bitcast.4.at_ref, bf16[1024,768]{1,0:T(8,128)(2,1)S(1)} %copy-done.1, bf16[1024,768]{1,0:T(8,128)(2,1)S(1)} %copy-done.1, bf16[1024,768]{1,0:T(8,128)(2,1)} %collective-permute-done.6.refs_2_, bf16[1024,256]{1,0:T(8,128)(2,1)S(1)} %copy-done.5, ...), custom_call_target="tpu_custom_call" | custom-call | flops 11960000512 | bytes 100000 | tf_op jit(solution)/shard_map/pallas_call | solution.py:143
  104.7 3.5 %collective-permute-done.13 = bf16[512,128]{1,0:T(8,128)(2,1)S(1)} collective-permute-done((bf16[512,128]{1,0:T(8,128)(2,1)S(1)}, bf16[512,128]{1,0:T(8,128)(2,1)S(1)}, u32[]{:S(2)}, u32[]{:S(2)}) %collective-permute-start.13) | collective-permute-done | bytes 131104 | tf_op jit(solution)/shard_map/ppermute | solution.py:208
  108.2 1.9 %collective-permute-start.16 = (bf16[512,256]{1,0:T(8,128)(2,1)S(1)}, bf16[512,256]{1,0:T(8,128)(2,1)S(1)}, u32[]{:S(2)}, u32[]{:S(2)}) collective-permute-start(bf16[512,256]{1,0:T(8,128)(2,1)S(1)} %constant_dynamic-update-slice_fusion.refs_6_.refs_0_), channel_id=1, source_target_pairs={{0,6},{2,0},{4,2},{6,4},{1,7},{3,1},{5,3},{7,5},{8,14},{10,8},{12,... | collective-permute-start | bytes 786440 | tf_op jit(solution)/shard_map/ppermute | solution.py:222
  110.8 6.9 %shard_map.86.refs_5_ = bf16[2,528,128]{2,1,0:T(8,128)(2,1)S(1)} custom-call(s32[1]{0:T(128)} %bitcast.4.at_ref, bf16[1024,128]{1,0:T(8,128)(2,1)} %collective-permute-done.5.refs_0_, bf16[1024,256]{1,0:T(8,128)(2,1)S(1)} %slice.21.refs_1_, bf16[1024,256]{1,0:T(8,128)(2,1)} %collective-permute-done.refs_2_, ...), custom_call_target="tpu_custom_call" | custom-call | flops 11960000512 | bytes 100000 | tf_op jit(solution)/shard_map/pallas_call | solution.py:143
  118.3 6.8 %shard_map.87.a = bf16[2,528,128]{2,1,0:T(8,128)(2,1)S(1)} custom-call(s32[1]{0:T(128)} %bitcast.4.at_ref, bf16[1024,128]{1,0:T(8,128)(2,1)S(1)} %slice.20.refs_0_, bf16[1024,256]{1,0:T(8,128)(2,1)S(1)} %slice.21.refs_1_, bf16[1024,256]{1,0:T(8,128)(2,1)} %collective-permute-done.refs_2_, bf16[1024,256]{1,0:T(8,128)(2,1)S(1)} %collective-permute-done.3.refs_3_, ...), custom_call_target="tpu_custom_call" | custom-call | flops 11960000512 | bytes 100000 | tf_op jit(solution)/shard_map/pallas_call | solution.py:143
  125.8 5.0 %collective-permute-done.17.refs_2_.refs_3_ = bf16[512,256]{1,0:T(8,128)(2,1)S(1)} collective-permute-done((bf16[512,256]{1,0:T(8,128)(2,1)S(1)}, bf16[512,256]{1,0:T(8,128)(2,1)S(1)}, u32[]{:S(2)}, u32[]{:S(2)}) %collective-permute-start.17) | collective-permute-done | bytes 262176 | tf_op jit(solution)/shard_map/ppermute | solution.py:223
  133.1 2.4 %collective-permute-start.24 = (bf16[512,256]{1,0:T(8,128)(2,1)S(1)}, bf16[512,256]{1,0:T(8,128)(2,1)S(1)}, u32[]{:S(2)}, u32[]{:S(2)}) collective-permute-start(bf16[512,256]{1,0:T(8,128)(2,1)S(1)} %constant_dynamic-update-slice_fusion.2.refs_6_.refs_0_), channel_id=1, source_target_pairs={{0,6},{2,0},{4,2},{6,4},{1,7},{3,1},{5,3},{7,5},{8,14},{10,8},{12,... | collective-permute-start | bytes 786440 | tf_op jit(solution)/shard_map/ppermute | solution.py:222
  135.9 4.0 %collective-permute-done.18 = bf16[512,128]{1,0:T(8,128)(2,1)S(1)} collective-permute-done((bf16[512,128]{1,0:T(8,128)(2,1)S(1)}, bf16[512,128]{1,0:T(8,128)(2,1)S(1)}, u32[]{:S(2)}, u32[]{:S(2)}) %collective-permute-start.18) | collective-permute-done | bytes 131104 | tf_op jit(solution)/shard_map/ppermute | solution.py:208
  140.6 6.5 %collective-permute-done.23.refs_7_.refs_1_ = bf16[512,256]{1,0:T(8,128)(2,1)S(1)} collective-permute-done((bf16[512,256]{1,0:T(8,128)(2,1)S(1)}, bf16[512,256]{1,0:T(8,128)(2,1)S(1)}, u32[]{:S(2)}, u32[]{:S(2)}) %collective-permute-start.23) | collective-permute-done | bytes 262176 | tf_op jit(solution)/shard_map/ppermute | solution.py:221
  147.1 4.6 %shard_map.91.refs_6_ = f32[512,1536]{1,0:T(8,128)S(1)} custom-call(s32[4]{0:T(128)S(1)} %pad_add_fusion.at_ref, bf16[512,256]{1,0:T(8,128)(2,1)S(1)} %constant_dynamic-update-slice_fusion.refs_6_.refs_0_, bf16[512,256]{1,0:T(8,128)(2,1)S(1)} %collective-permute-done.15.refs_0_.refs_1_, bf16[512,256]{1,0:T(8,128)(2,1)S(1)} %collective-permute-done.16.refs_1_.refs_2_, ...), custom_call_target="tpu_custom_call" | custom-call | flops 5520000000 | bytes 100000 | tf_op jit(solution)/shard_map/pallas_call | solution.py:291
  151.8 4.6 %shard_map.92.refs_6_ = f32[512,1536]{1,0:T(8,128)S(1)} custom-call(s32[4]{0:T(128)S(1)} %pad_add_fusion.at_ref, bf16[512,256]{1,0:T(8,128)(2,1)S(1)} %constant_dynamic-update-slice_fusion.2.refs_6_.refs_0_, bf16[512,256]{1,0:T(8,128)(2,1)S(1)} %collective-permute-done.23.refs_7_.refs_1_, bf16[512,256]{1,0:T(8,128)(2,1)S(1)} %collective-permute-done.24.refs_8_.refs_2_, ...), custom_call_target="tpu_custom_call" | custom-call | flops 5520000000 | bytes 100000 | tf_op jit(solution)/shard_map/pallas_call | solution.py:291
  158.1 4.6 %shard_map.93 = (bf16[512,384]{1,0:T(8,128)(2,1)S(1)}, bf16[512,384]{1,0:T(8,128)(2,1)S(1)}, bf16[512,384]{1,0:T(8,128)(2,1)S(1)}, bf16[512,384]{1,0:T(8,128)(2,1)S(1)}) custom-call(s32[4]{0:T(128)S(1)} %pad_add_fusion.at_ref, bf16[512,256]{1,0:T(8,128)(2,1)S(1)} %constant_dynamic-update-slice_fusion.4.refs_6_.refs_0_, ...), custom_call_target="tpu_custom_call" | custom-call | flops 5520000000 | bytes 100000 | tf_op jit(solution)/shard_map/pallas_call | solution.py:291
  164.4 1.8 collective-permute-start.27
  167.4 6.0 %collective-permute-done.26 = bf16[512,384]{1,0:T(8,128)(2,1)S(1)} collective-permute-done((bf16[512,384]{1,0:T(8,128)(2,1)S(1)}, bf16[512,384]{1,0:T(8,128)(2,1)S(1)}, u32[]{:S(2)}, u32[]{:S(2)}) %collective-permute-start.26) | collective-permute-done | bytes 393248 | tf_op jit(solution)/shard_map/ppermute | solution.py:200
  173.5 10.1 %collective-permute-done.28 = bf16[512,384]{1,0:T(8,128)(2,1)S(1)} collective-permute-done((bf16[512,384]{1,0:T(8,128)(2,1)S(1)}, bf16[512,384]{1,0:T(8,128)(2,1)S(1)}, u32[]{:S(2)}, u32[]{:S(2)}) %collective-permute-start.28) | collective-permute-done | bytes 393248 | tf_op jit(solution)/shard_map/ppermute | solution.py:200
  (85 shorter events, 25.2 us)
Async XLA Ops:
  3.5 28.8 %all-to-all-start = ((bf16[16,64,768]{2,1,0:T(8,128)(2,1)}), bf16[16,64,768]{2,1,0:T(8,128)(2,1)S(1)}, u32[]{:S(2)}, u32[]{:S(2)}) async-start(bf16[16,64,768]{2,1,0:T(8,128)(2,1)} %shard_map.73.refs_0_.token_ref), calls=%async_computation | async-start | bytes 3145728 | tf_op jit(solution)/shard_map/all_to_all | solution.py:319
  33.6 34.8 %collective-permute-start.6 = (bf16[1024,768]{1,0:T(8,128)(2,1)}, bf16[1024,768]{1,0:T(8,128)(2,1)}, u32[]{:S(2)}, u32[]{:S(2)}) collective-permute-start(bf16[1024,768]{1,0:T(8,128)(2,1)} %shard_map.76.refs_1_.refs_0_), channel_id=1, source_target_pairs={{0,1},{1,0},{2,3},{3,2},{4,5},{5,4},{6,7},{7,6},{8,9},{9,8},{10,11... | collective-permute-start | bytes 4718600 | tf_op jit(solution)/shard_map/ppermute | solution.py:204
  38.6 13.6 %collective-permute-start.1 = (bf16[1024,256]{1,0:T(8,128)(2,1)S(1)}, bf16[1024,256]{1,0:T(8,128)(2,1)S(1)}, u32[]{:S(2)}, u32[]{:S(2)}) collective-permute-start(bf16[1024,256]{1,0:T(8,128)(2,1)S(1)} %get-tuple-element.28), channel_id=1, source_target_pairs={{0,16},{16,0},{32,48},{48,32},{1,17},{17,1},{33,49},{49,33},{2,18}... | collective-permute-start | bytes 1572872 | tf_op jit(solution)/shard_map/ppermute | solution.py:212
  39.8 17.2 %all-to-all-start.1 = ((bf16[16,64,384]{2,1,0:T(8,128)(2,1)}), bf16[16,64,384]{2,1,0:T(8,128)(2,1)S(1)}, u32[]{:S(2)}, u32[]{:S(2)}) async-start(bf16[16,64,384]{2,1,0:T(8,128)(2,1)} %shard_map.77), calls=%async_computation.1 | async-start | bytes 1572864 | tf_op jit(solution)/shard_map/all_to_all | solution.py:319
  53.0 13.0 %collective-permute-start.2 = (bf16[1024,256]{1,0:T(8,128)(2,1)}, bf16[1024,256]{1,0:T(8,128)(2,1)S(1)}, u32[]{:S(2)}, u32[]{:S(2)}) collective-permute-start(bf16[1024,256]{1,0:T(8,128)(2,1)} %shard_map.78), channel_id=1, source_target_pairs={{0,16},{16,0},{32,48},{48,32},{1,17},{17,1},{33,49},{49,33},{2,18}... | collective-permute-start | bytes 1572872 | tf_op jit(solution)/shard_map/ppermute | solution.py:212
  54.2 14.3 %collective-permute-start.8 = (bf16[1024,256]{1,0:T(8,128)(2,1)}, bf16[1024,256]{1,0:T(8,128)(2,1)}, u32[]{:S(2)}, u32[]{:S(2)}) collective-permute-start(bf16[1024,256]{1,0:T(8,128)(2,1)} %copy-done.6), channel_id=1, source_target_pairs={{0,1},{1,0},{2,3},{3,2},{4,5},{5,4},{6,7},{7,6},{8,9},{9,8},{10,11... | collective-permute-start | bytes 1572872 | tf_op jit(solution)/shard_map/ppermute | solution.py:204
  55.2 22.3 %collective-permute-start.9 = (bf16[1024,256]{1,0:T(8,128)(2,1)}, bf16[1024,256]{1,0:T(8,128)(2,1)}, u32[]{:S(2)}, u32[]{:S(2)}) collective-permute-start(bf16[1024,256]{1,0:T(8,128)(2,1)} %get-tuple-element.27), channel_id=1, source_target_pairs={{0,48},{48,0},{16,32},{32,16},{1,49},{49,1},{17,33},{33,17},{2,50}... | collective-permute-start | bytes 1572872 | tf_op jit(solution)/shard_map/ppermute | solution.py:216
  58.0 52.8 %collective-permute-start = (bf16[1024,256]{1,0:T(8,128)(2,1)S(1)}, bf16[1024,256]{1,0:T(8,128)(2,1)}, u32[]{:S(2)}, u32[]{:S(2)}) collective-permute-start(bf16[1024,256]{1,0:T(8,128)(2,1)S(1)} %slice.21.refs_1_), channel_id=1, source_target_pairs={{0,1},{1,0},{2,3},{3,2},{4,5},{5,4},{6,7},{7,6},{8,9},{9,8},{10,11... | collective-permute-start | bytes 1572872 | tf_op jit(solution)/shard_map/ppermute | solution.py:204
  60.0 72.0 %all-to-all-start.2 = ((bf16[4,384,1536]{2,1,0:T(8,128)(2,1)}), bf16[4,384,1536]{2,1,0:T(8,128)(2,1)}, u32[]{:S(2)}, u32[]{:S(2)}) async-start(bf16[4,384,1536]{2,1,0:T(8,128)(2,1)} %shard_map.89), calls=%async_computation.2 | async-start | bytes 9437184 | tf_op jit(solution)/shard_map/all_to_all | solution.py:339
  65.9 44.2 %collective-permute-start.5 = (bf16[1024,128]{1,0:T(8,128)(2,1)S(1)}, bf16[1024,128]{1,0:T(8,128)(2,1)}, u32[]{:S(2)}, u32[]{:S(2)}) collective-permute-start(bf16[1024,128]{1,0:T(8,128)(2,1)S(1)} %slice.20.refs_0_), channel_id=1, source_target_pairs={{0,48},{48,0},{16,32},{32,16},{1,49},{49,1},{17,33},{33,17},{2,50}... | collective-permute-start | bytes 786440 | tf_op jit(solution)/shard_map/ppermute | solution.py:216
  68.4 26.1 %collective-permute-start.3 = (bf16[1024,256]{1,0:T(8,128)(2,1)}, bf16[1024,256]{1,0:T(8,128)(2,1)S(1)}, u32[]{:S(2)}, u32[]{:S(2)}) collective-permute-start(bf16[1024,256]{1,0:T(8,128)(2,1)} %shard_map.79), channel_id=1, source_target_pairs={{0,16},{16,0},{32,48},{48,32},{1,17},{17,1},{33,49},{49,33},{2,18}... | collective-permute-start | bytes 1572872 | tf_op jit(solution)/shard_map/ppermute | solution.py:212
  68.4 17.5 %collective-permute-start.7 = (bf16[1024,256]{1,0:T(8,128)(2,1)}, bf16[1024,256]{1,0:T(8,128)(2,1)S(1)}, u32[]{:S(2)}, u32[]{:S(2)}) collective-permute-start(bf16[1024,256]{1,0:T(8,128)(2,1)} %copy-done.4), channel_id=1, source_target_pairs={{0,1},{1,0},{2,3},{3,2},{4,5},{5,4},{6,7},{7,6},{8,9},{9,8},{10,11... | collective-permute-start | bytes 1572872 | tf_op jit(solution)/shard_map/ppermute | solution.py:204
  84.6 10.5 %collective-permute-start.10 = (bf16[2,528,128]{2,1,0:T(8,128)(2,1)S(1)}, bf16[2,528,128]{2,1,0:T(8,128)(2,1)S(1)}, u32[]{:S(2)}, u32[]{:S(2)}) collective-permute-start(bf16[2,528,128]{2,1,0:T(8,128)(2,1)S(1)} %shard_map.81.refs_5_), channel_id=1, source_target_pairs={{0,48},{48,0},{16,32},{32,16},{1,49},{49,1},{17,33},{33,17},{2,50}... | collective-permute-start | bytes 811016 | tf_op jit(solution)/shard_map/ppermute | solution.py:216
  92.8 9.9 %collective-permute-start.11 = (bf16[2,528,128]{2,1,0:T(8,128)(2,1)S(1)}, bf16[2,528,128]{2,1,0:T(8,128)(2,1)S(1)}, u32[]{:S(2)}, u32[]{:S(2)}) collective-permute-start(bf16[2,528,128]{2,1,0:T(8,128)(2,1)S(1)} %shard_map.82.refs_0_), channel_id=1, source_target_pairs={{0,48},{48,0},{16,32},{32,16},{1,49},{49,1},{17,33},{33,17},{2,50}... | collective-permute-start | bytes 811016 | tf_op jit(solution)/shard_map/ppermute | solution.py:216
  94.5 16.3 %collective-permute-start.4 = (bf16[1024,256]{1,0:T(8,128)(2,1)S(1)}, bf16[1024,256]{1,0:T(8,128)(2,1)S(1)}, u32[]{:S(2)}, u32[]{:S(2)}) collective-permute-start(bf16[1024,256]{1,0:T(8,128)(2,1)S(1)} %collective-permute-done.3.refs_3_), channel_id=1, source_target_pairs={{0,1},{1,0},{2,3},{3,2},{4,5},{5,4},{6,7},{7,6},{8,9},{9,8},{10,11... | collective-permute-start | bytes 1572872 | tf_op jit(solution)/shard_map/ppermute | solution.py:204
  95.5 9.0 %collective-permute-start.12 = (bf16[512,128]{1,0:T(8,128)(2,1)S(1)}, bf16[512,128]{1,0:T(8,128)(2,1)S(1)}, u32[]{:S(2)}, u32[]{:S(2)}) collective-permute-start(bf16[512,128]{1,0:T(8,128)(2,1)S(1)} %get-tuple-element.17), channel_id=1, source_target_pairs={{0,64},{64,0},{1,65},{65,1},{2,66},{66,2},{3,67},{67,3},{4,68},{68... | collective-permute-start | bytes 393224 | tf_op jit(solution)/shard_map/ppermute | solution.py:208
  103.2 5.0 %collective-permute-start.13 = (bf16[512,128]{1,0:T(8,128)(2,1)S(1)}, bf16[512,128]{1,0:T(8,128)(2,1)S(1)}, u32[]{:S(2)}, u32[]{:S(2)}) collective-permute-start(bf16[512,128]{1,0:T(8,128)(2,1)S(1)} %get-tuple-element.18), channel_id=1, source_target_pairs={{0,64},{64,0},{1,65},{65,1},{2,66},{66,2},{3,67},{67,3},{4,68},{68... | collective-permute-start | bytes 393224 | tf_op jit(solution)/shard_map/ppermute | solution.py:208
  104.6 21.3 %collective-permute-start.15 = (bf16[512,256]{1,0:T(8,128)(2,1)S(1)}, bf16[512,256]{1,0:T(8,128)(2,1)S(1)}, u32[]{:S(2)}, u32[]{:S(2)}) collective-permute-start(bf16[512,256]{1,0:T(8,128)(2,1)S(1)} %constant_dynamic-update-slice_fusion.refs_6_.refs_0_), channel_id=1, source_target_pairs={{0,2},{2,4},{4,6},{6,0},{1,3},{3,5},{5,7},{7,1},{8,10},{10,12},{12... | collective-permute-start | bytes 786440 | tf_op jit(solution)/shard_map/ppermute | solution.py:221
  108.2 17.6 %collective-permute-start.16 = (bf16[512,256]{1,0:T(8,128)(2,1)S(1)}, bf16[512,256]{1,0:T(8,128)(2,1)S(1)}, u32[]{:S(2)}, u32[]{:S(2)}) collective-permute-start(bf16[512,256]{1,0:T(8,128)(2,1)S(1)} %constant_dynamic-update-slice_fusion.refs_6_.refs_0_), channel_id=1, source_target_pairs={{0,6},{2,0},{4,2},{6,4},{1,7},{3,1},{5,3},{7,5},{8,14},{10,8},{12,... | collective-permute-start | bytes 786440 | tf_op jit(solution)/shard_map/ppermute | solution.py:222
  110.1 20.7 %collective-permute-start.17 = (bf16[512,256]{1,0:T(8,128)(2,1)S(1)}, bf16[512,256]{1,0:T(8,128)(2,1)S(1)}, u32[]{:S(2)}, u32[]{:S(2)}) collective-permute-start(bf16[512,256]{1,0:T(8,128)(2,1)S(1)} %constant_dynamic-update-slice_fusion.refs_6_.refs_0_), channel_id=1, source_target_pairs={{0,4},{2,6},{4,0},{6,2},{1,5},{3,7},{5,1},{7,3},{8,12},{10,14},{12... | collective-permute-start | bytes 786440 | tf_op jit(solution)/shard_map/ppermute | solution.py:223
  117.6 13.2 %collective-permute-start.14 = (bf16[2,528,128]{2,1,0:T(8,128)(2,1)S(1)}, bf16[2,528,128]{2,1,0:T(8,128)(2,1)S(1)}, u32[]{:S(2)}, u32[]{:S(2)}) collective-permute-start(bf16[2,528,128]{2,1,0:T(8,128)(2,1)S(1)} %shard_map.86.refs_5_), channel_id=1, source_target_pairs={{0,48},{48,0},{16,32},{32,16},{1,49},{49,1},{17,33},{33,17},{2,50}... | collective-permute-start | bytes 811016 | tf_op jit(solution)/shard_map/ppermute | solution.py:216
  132.0 15.2 %collective-permute-start.22 = (bf16[4,384,1536]{2,1,0:T(8,128)(2,1)}, bf16[4,384,1536]{2,1,0:T(8,128)(2,1)}, u32[]{:S(2)}, u32[]{:S(2)}) collective-permute-start(bf16[4,384,1536]{2,1,0:T(8,128)(2,1)} %shard_map.90.refs_4_), channel_id=1, source_target_pairs={{0,1},{1,0},{2,3},{3,2},{4,5},{5,4},{6,7},{7,6},{8,9},{9,8},{10,11... | collective-permute-start | bytes 14155784 | tf_op jit(solution)/shard_map/ppermute | solution.py:204
  132.8 14.3 %collective-permute-start.23 = (bf16[512,256]{1,0:T(8,128)(2,1)S(1)}, bf16[512,256]{1,0:T(8,128)(2,1)S(1)}, u32[]{:S(2)}, u32[]{:S(2)}) collective-permute-start(bf16[512,256]{1,0:T(8,128)(2,1)S(1)} %constant_dynamic-update-slice_fusion.2.refs_6_.refs_0_), channel_id=1, source_target_pairs={{0,2},{2,4},{4,6},{6,0},{1,3},{3,5},{5,7},{7,1},{8,10},{10,12},{12... | collective-permute-start | bytes 786440 | tf_op jit(solution)/shard_map/ppermute | solution.py:221
  133.1 14.0 %collective-permute-start.24 = (bf16[512,256]{1,0:T(8,128)(2,1)S(1)}, bf16[512,256]{1,0:T(8,128)(2,1)S(1)}, u32[]{:S(2)}, u32[]{:S(2)}) collective-permute-start(bf16[512,256]{1,0:T(8,128)(2,1)S(1)} %constant_dynamic-update-slice_fusion.2.refs_6_.refs_0_), channel_id=1, source_target_pairs={{0,6},{2,0},{4,2},{6,4},{1,7},{3,1},{5,3},{7,5},{8,14},{10,8},{12,... | collective-permute-start | bytes 786440 | tf_op jit(solution)/shard_map/ppermute | solution.py:222
  135.5 11.6 %collective-permute-start.25 = (bf16[512,256]{1,0:T(8,128)(2,1)S(1)}, bf16[512,256]{1,0:T(8,128)(2,1)S(1)}, u32[]{:S(2)}, u32[]{:S(2)}) collective-permute-start(bf16[512,256]{1,0:T(8,128)(2,1)S(1)} %constant_dynamic-update-slice_fusion.2.refs_6_.refs_0_), channel_id=1, source_target_pairs={{0,4},{2,6},{4,0},{6,2},{1,5},{3,7},{5,1},{7,3},{8,12},{10,14},{12... | collective-permute-start | bytes 786440 | tf_op jit(solution)/shard_map/ppermute | solution.py:223
  135.5 4.4 %collective-permute-start.18 = (bf16[512,128]{1,0:T(8,128)(2,1)S(1)}, bf16[512,128]{1,0:T(8,128)(2,1)S(1)}, u32[]{:S(2)}, u32[]{:S(2)}) collective-permute-start(bf16[512,128]{1,0:T(8,128)(2,1)S(1)} %get-tuple-element.20), channel_id=1, source_target_pairs={{0,64},{64,0},{1,65},{65,1},{2,66},{66,2},{3,67},{67,3},{4,68},{68... | collective-permute-start | bytes 393224 | tf_op jit(solution)/shard_map/ppermute | solution.py:208
  139.9 16.4 %collective-permute-start.19 = (bf16[512,256]{1,0:T(8,128)(2,1)S(1)}, bf16[512,256]{1,0:T(8,128)(2,1)S(1)}, u32[]{:S(2)}, u32[]{:S(2)}) collective-permute-start(bf16[512,256]{1,0:T(8,128)(2,1)S(1)} %constant_dynamic-update-slice_fusion.4.refs_6_.refs_0_), channel_id=1, source_target_pairs={{0,2},{2,4},{4,6},{6,0},{1,3},{3,5},{5,7},{7,1},{8,10},{10,12},{12... | collective-permute-start | bytes 786440 | tf_op jit(solution)/shard_map/ppermute | solution.py:221
  147.1 9.3 %collective-permute-start.20 = (bf16[512,256]{1,0:T(8,128)(2,1)S(1)}, bf16[512,256]{1,0:T(8,128)(2,1)S(1)}, u32[]{:S(2)}, u32[]{:S(2)}) collective-permute-start(bf16[512,256]{1,0:T(8,128)(2,1)S(1)} %constant_dynamic-update-slice_fusion.4.refs_6_.refs_0_), channel_id=1, source_target_pairs={{0,6},{2,0},{4,2},{6,4},{1,7},{3,1},{5,3},{7,5},{8,14},{10,8},{12,... | collective-permute-start | bytes 786440 | tf_op jit(solution)/shard_map/ppermute | solution.py:222
  147.1 11.0 %collective-permute-start.21 = (bf16[512,256]{1,0:T(8,128)(2,1)S(1)}, bf16[512,256]{1,0:T(8,128)(2,1)S(1)}, u32[]{:S(2)}, u32[]{:S(2)}) collective-permute-start(bf16[512,256]{1,0:T(8,128)(2,1)S(1)} %constant_dynamic-update-slice_fusion.4.refs_6_.refs_0_), channel_id=1, source_target_pairs={{0,4},{2,6},{4,0},{6,2},{1,5},{3,7},{5,1},{7,3},{8,12},{10,14},{12... | collective-permute-start | bytes 786440 | tf_op jit(solution)/shard_map/ppermute | solution.py:223
  162.7 10.7 %collective-permute-start.26 = (bf16[512,384]{1,0:T(8,128)(2,1)S(1)}, bf16[512,384]{1,0:T(8,128)(2,1)S(1)}, u32[]{:S(2)}, u32[]{:S(2)}) collective-permute-start(bf16[512,384]{1,0:T(8,128)(2,1)S(1)} %get-tuple-element.22), channel_id=1, source_target_pairs={{0,8},{1,9},{8,0},{9,1},{2,10},{3,11},{10,2},{11,3},{4,12},{5,13},... | collective-permute-start | bytes 1179656 | tf_op jit(solution)/shard_map/ppermute | solution.py:200
  164.4 9.1 %collective-permute-start.27 = (bf16[512,384]{1,0:T(8,128)(2,1)S(1)}, bf16[512,384]{1,0:T(8,128)(2,1)S(1)}, u32[]{:S(2)}, u32[]{:S(2)}) collective-permute-start(bf16[512,384]{1,0:T(8,128)(2,1)S(1)} %get-tuple-element.23), channel_id=1, source_target_pairs={{0,1},{1,0},{2,3},{3,2},{4,5},{5,4},{6,7},{7,6},{8,9},{9,8},{10,11... | collective-permute-start | bytes 1179656 | tf_op jit(solution)/shard_map/ppermute | solution.py:204
  166.1 17.5 %collective-permute-start.28 = (bf16[512,384]{1,0:T(8,128)(2,1)S(1)}, bf16[512,384]{1,0:T(8,128)(2,1)S(1)}, u32[]{:S(2)}, u32[]{:S(2)}) collective-permute-start(bf16[512,384]{1,0:T(8,128)(2,1)S(1)} %get-tuple-element.24), channel_id=1, source_target_pairs={{0,9},{1,8},{8,1},{9,0},{2,11},{3,10},{10,3},{11,2},{4,13},{5,12},... | collective-permute-start | bytes 1179656 | tf_op jit(solution)/shard_map/ppermute | solution.py:200
  (9 other events, 41.6 us)
where the time goes:
time: 186 us; the launch traced here: 185 us
  Pallas kernels  67.8 us (36%)
  waiting for transfers between devices  59 us (32%)
  starting transfers between devices  50.2 us (27%)
  local copies, waits for them, and re-layouts  7.26 us (4%)
    pallas_call x6, Pallas kernels, attend(): pl.pallas_call(functools.partial(attend_kernel, pieces=pieces, queries=n,...  41.4 us
    ppermute x2, waiting for transfers between devices, opposite_y(): return lax.ppermute(a, ('yhi', 'core'), perm)  16.1 us
    pallas_call x3, Pallas kernels, project(): pl.pallas_call(functools.partial(project_kernel, head=head, before=len(be...  13.8 us
    all_to_all x2, starting transfers between devices, exchange(): a = lax.all_to_all(a, every, split_axis=0, concat_axis=0, tiled=True)  13 us
    all_to_all x2, waiting for transfers between devices, exchange(): a = lax.all_to_all(a, every, split_axis=0, concat_axis=0, tiled=True)  12.5 us
    ppermute x7, starting transfers between devices, swap(): return lax.ppermute(a, 'core', [(0, 1), (1, 0)])  10.8 us
    ppermute x3, waiting for transfers between devices, key_pair(): return lax.ppermute(a, 'x', [(0, 1), (1, 0), (2, 3), (3, 2)])  8.77 us
    ppermute x5, starting transfers between devices, query_pair(): return lax.ppermute(a, 'x', [(0, 3), (3, 0), (1, 2), (2, 1)])  7.99 us
  transfers between devices with their start and end apart: 32, of which 11 were waited for; matrix products, arithmetic and copies ran while one was open for 2% of the time, Pallas kernels for 32%

commit v1 on v0

--- a/solution.py
+++ b/solution.py
@@ -308,8 +308,29 @@
     )(at, *blocks, *weights, *before, *tokens)
 
 
+def finish_kernel(core_ref, a, b, c, d, o_ref):
+    own = (a[...].astype(F32) + b[...].astype(F32)).astype(BF)
+    other = (c[...].astype(F32) + d[...].astype(F32)).astype(BF)
+    tok = o_ref.shape[2]
+    for i in range(o_ref.shape[0]):
+        rows = slice(i * tok, (i + 1) * tok)
+        o_ref[i, core_ref[0]] = own[rows]
+        o_ref[i, 1 - core_ref[0]] = other[rows]
+
+
+def finish(core, tok, *terms):
+    rows, cols = terms[0].shape
+    vmem = pl.BlockSpec(memory_space=pltpu.VMEM)
+    return pl.pallas_call(
+        finish_kernel,
+        in_specs=[pl.BlockSpec(memory_space=pltpu.SMEM)] + [vmem] * 4,
+        out_shape=jax.ShapeDtypeStruct((rows // tok, 2, tok, cols), BF),
+        compiler_params=params(12),
+        cost_estimate=cost(1),
+    )(core, *terms).reshape(2 * rows, cols)
+
+
 def on_device(q_vals, k_vals, v_vals, q_scale, k_scale, v_scale, out_weight):
-    cols = out_weight.shape[0]
     tok = q_vals.shape[0]
     ylo, yhi, z, core = (lax.axis_index(n) for n in ("ylo", "yhi", "z", "core"))
     mine = ylo.reshape(1)
@@ -372,12 +393,9 @@
     out = project(at, 0, set0, weights, tokens=(both2, *set1[1:]))
     out = project(at, 1, set1, weights, (out,))
     out = project(at, 2, set2, weights, (out,), last=True)
-    own = out[2].astype(F32) + opposite_y(out[0]).astype(F32)
-    other = swap(out[3]).astype(F32) + opposite_y(out[1], flip=True).astype(F32)
-    own, other = own.astype(BF), other.astype(BF)
-    one = jnp.where(core == 0, own, other).reshape(-1, tok, cols)
-    two = jnp.where(core == 0, other, own).reshape(-1, tok, cols)
-    return jnp.stack([one, two], axis=1).reshape(-1, cols)
+    return finish(
+        core.reshape(1), tok, out[2], opposite_y(out[0]), swap(out[3]), opposite_y(out[1], flip=True)
+    )
 
 
 def solution(mesh):

time: 186 us -> 185 us (level)
  no operation moved by 1% of the time
where the time goes in v1:
time: 185 us
  Pallas kernels  68.8 us (37%)
  waiting for transfers between devices  59 us (32%)
  starting transfers between devices  50.2 us (27%)
  local copies, waits for them, and re-layouts  6.27 us (3%)
    pallas_call x6, Pallas kernels, attend(): pl.pallas_call(functools.partial(attend_kernel, pieces=pieces, queries=n,...  41.4 us
    ppermute x2, waiting for transfers between devices, opposite_y(): return lax.ppermute(a, ('yhi', 'core'), perm)  16.1 us
    pallas_call x3, Pallas kernels, project(): pl.pallas_call(functools.partial(project_kernel, head=head, before=len(be...  13.8 us
    all_to_all x2, starting transfers between devices, exchange(): a = lax.all_to_all(a, every, split_axis=0, concat_axis=0, tiled=True)  13 us
    all_to_all x2, waiting for transfers between devices, exchange(): a = lax.all_to_all(a, every, split_axis=0, concat_axis=0, tiled=True)  12.5 us
    ppermute x7, starting transfers between devices, swap(): return lax.ppermute(a, 'core', [(0, 1), (1, 0)])  10.8 us
    ppermute x3, waiting for transfers between devices, key_pair(): return lax.ppermute(a, 'x', [(0, 1), (1, 0), (2, 3), (3, 2)])  8.79 us
    ppermute x5, starting transfers between devices, query_pair(): return lax.ppermute(a, 'x', [(0, 3), (3, 0), (1, 2), (2, 1)])  8 us
  transfers between devices with their start and end apart: 32, of which 11 were waited for; matrix products, arithmetic and copies ran while one was open for 2% of the time, Pallas kernels for 32%

profile of v1, /device:TPU:1, one launch (start us, length us, event | category | flops | bytes accessed | tf_op | source)
XLA Modules:
  0.0 184.6 jit_solution(12750256997485379180)
XLA Ops:
  0.0 3.5 %shard_map.73.refs_0_.token_ref = bf16[16,64,768]{2,1,0:T(8,128)(2,1)} custom-call(bf16[64,6144]{1,0:T(8,128)(2,1)} %q_ref.3, bf16[64,6144]{1,0:T(8,128)(2,1)} %k_ref.3, bf16[64,6144]{1,0:T(8,128)(2,1)} %v_ref.3, bf16[48,64]{1,0:T(8,128)(2,1)} %bitcast.15, bf16[48,64]{1,0:T(8,128)(2,1)} %bitcast.17, bf16[48,64]{1,0:T(8,128)(2,1)} %bitcast.19), custom_call_target="tpu_custom_call" | custom-call | flops 5520000000 | bytes 100000 | tf_op jit(solution)/shard_map/pallas_call | solution.py:64
  3.5 8.6 %all-to-all-start = ((bf16[16,64,768]{2,1,0:T(8,128)(2,1)}), bf16[16,64,768]{2,1,0:T(8,128)(2,1)S(1)}, u32[]{:S(2)}, u32[]{:S(2)}) async-start(bf16[16,64,768]{2,1,0:T(8,128)(2,1)} %shard_map.73.refs_0_.token_ref), calls=%async_computation | async-start | bytes 3145728 | tf_op jit(solution)/shard_map/all_to_all | solution.py:340
  12.1 3.0 %shard_map.74.refs_1_.refs_0_ = bf16[16,64,384]{2,1,0:T(8,128)(2,1)} custom-call(bf16[64,6144]{1,0:T(8,128)(2,1)} %q_ref.3, bf16[64,6144]{1,0:T(8,128)(2,1)} %k_ref.3, bf16[64,6144]{1,0:T(8,128)(2,1)} %v_ref.3, bf16[48,64]{1,0:T(8,128)(2,1)} %bitcast.16, bf16[48,64]{1,0:T(8,128)(2,1)} %bitcast.18, bf16[48,64]{1,0:T(8,128)(2,1)} %bitcast.20, ...), custom_call_target="tpu_custom_call" | custom-call | flops 5520000000 | bytes 100000 | tf_op jit(solution)/shard_map/pallas_call | solution.py:64
  15.1 4.8 %shard_map.75.refs_2_.refs_0_ = bf16[4,384,1536]{2,1,0:T(8,128)(2,1)} custom-call(bf16[384,6144]{1,0:T(8,128)(2,1)} %w_ref.1, bf16[16,64,768]{2,1,0:T(8,128)(2,1)} %shard_map.73.refs_0_.token_ref), custom_call_target="tpu_custom_call" | custom-call | flops 7360000000 | bytes 100000 | tf_op jit(solution)/shard_map/pallas_call | solution.py:238
  19.9 12.5 %all-to-all-done = bf16[16,64,768]{2,1,0:T(8,128)(2,1)S(1)} async-done(((bf16[16,64,768]{2,1,0:T(8,128)(2,1)}), bf16[16,64,768]{2,1,0:T(8,128)(2,1)S(1)}, u32[]{:S(2)}, u32[]{:S(2)}) %all-to-all-start) | async-done | bytes 1572896 | tf_op jit(solution)/shard_map/all_to_all | solution.py:340
  33.6 2.5 %collective-permute-start.6 = (bf16[1024,768]{1,0:T(8,128)(2,1)}, bf16[1024,768]{1,0:T(8,128)(2,1)}, u32[]{:S(2)}, u32[]{:S(2)}) collective-permute-start(bf16[1024,768]{1,0:T(8,128)(2,1)} %shard_map.76.refs_1_.refs_0_), channel_id=1, source_target_pairs={{0,1},{1,0},{2,3},{3,2},{4,5},{5,4},{6,7},{7,6},{8,9},{9,8},{10,11... | collective-permute-start | bytes 4718600 | tf_op jit(solution)/shard_map/ppermute | solution.py:204
  36.1 2.5 %fusion = (bf16[1024,256]{1,0:T(8,128)(2,1)}, bf16[1024,256]{1,0:T(8,128)(2,1)S(1)}, bf16[1024,256]{1,0:T(8,128)(2,1)}) fusion(bf16[1024,768]{1,0:T(8,128)(2,1)} %shard_map.76.refs_1_.refs_0_), kind=kLoop, calls=%fused_computation.7 | loop fusion | bytes 3145728 | tf_op jit(solution)/shard_map/slice | solution.py:348
  39.8 4.4 %all-to-all-start.1 = ((bf16[16,64,384]{2,1,0:T(8,128)(2,1)}), bf16[16,64,384]{2,1,0:T(8,128)(2,1)S(1)}, u32[]{:S(2)}, u32[]{:S(2)}) async-start(bf16[16,64,384]{2,1,0:T(8,128)(2,1)} %shard_map.77), calls=%async_computation.1 | async-start | bytes 1572864 | tf_op jit(solution)/shard_map/all_to_all | solution.py:340
  44.3 7.9 %collective-permute-done.1.refs_1_.refs_3_ = bf16[1024,256]{1,0:T(8,128)(2,1)S(1)} collective-permute-done((bf16[1024,256]{1,0:T(8,128)(2,1)S(1)}, bf16[1024,256]{1,0:T(8,128)(2,1)S(1)}, u32[]{:S(2)}, u32[]{:S(2)}) %collective-permute-start.1) | collective-permute-done | bytes 524320 | tf_op jit(solution)/shard_map/ppermute | solution.py:212
  55.2 1.8 collective-permute-start.9
  58.0 1.9 %collective-permute-start = (bf16[1024,256]{1,0:T(8,128)(2,1)S(1)}, bf16[1024,256]{1,0:T(8,128)(2,1)}, u32[]{:S(2)}, u32[]{:S(2)}) collective-permute-start(bf16[1024,256]{1,0:T(8,128)(2,1)S(1)} %slice.21.refs_1_), channel_id=1, source_target_pairs={{0,1},{1,0},{2,3},{3,2},{4,5},{5,4},{6,7},{7,6},{8,9},{9,8},{10,11... | collective-permute-start | bytes 1572872 | tf_op jit(solution)/shard_map/ppermute | solution.py:204
  60.0 5.1 %all-to-all-start.2 = ((bf16[4,384,1536]{2,1,0:T(8,128)(2,1)}), bf16[4,384,1536]{2,1,0:T(8,128)(2,1)}, u32[]{:S(2)}, u32[]{:S(2)}) async-start(bf16[4,384,1536]{2,1,0:T(8,128)(2,1)} %shard_map.89), calls=%async_computation.2 | async-start | bytes 9437184 | tf_op jit(solution)/shard_map/all_to_all | solution.py:360
  65.9 2.5 %collective-permute-start.5 = (bf16[1024,128]{1,0:T(8,128)(2,1)S(1)}, bf16[1024,128]{1,0:T(8,128)(2,1)}, u32[]{:S(2)}, u32[]{:S(2)}) collective-permute-start(bf16[1024,128]{1,0:T(8,128)(2,1)S(1)} %slice.20.refs_0_), channel_id=1, source_target_pairs={{0,48},{48,0},{16,32},{32,16},{1,49},{49,1},{17,33},{33,17},{2,50}... | collective-permute-start | bytes 786440 | tf_op jit(solution)/shard_map/ppermute | solution.py:216
  68.4 2.1 %collective-permute-start.7 = (bf16[1024,256]{1,0:T(8,128)(2,1)}, bf16[1024,256]{1,0:T(8,128)(2,1)S(1)}, u32[]{:S(2)}, u32[]{:S(2)}) collective-permute-start(bf16[1024,256]{1,0:T(8,128)(2,1)} %copy-done.4), channel_id=1, source_target_pairs={{0,1},{1,0},{2,3},{3,2},{4,5},{5,4},{6,7},{7,6},{8,9},{9,8},{10,11... | collective-permute-start | bytes 1572872 | tf_op jit(solution)/shard_map/ppermute | solution.py:204
  70.5 7.0 %shard_map.80.refs_5_.a = bf16[2,528,128]{2,1,0:T(8,128)(2,1)S(1)} custom-call(s32[1]{0:T(128)} %bitcast.4.at_ref, bf16[1024,768]{1,0:T(8,128)(2,1)S(1)} %copy-done.1, bf16[1024,768]{1,0:T(8,128)(2,1)S(1)} %copy-done.1, bf16[1024,768]{1,0:T(8,128)(2,1)} %collective-permute-done.6.refs_2_, bf16[1024,256]{1,0:T(8,128)(2,1)S(1)} %copy-done.7, ...), custom_call_target="tpu_custom_call" | custom-call | flops 11960000512 | bytes 100000 | tf_op jit(solution)/shard_map/pallas_call | solution.py:143
  77.5 7.1 %shard_map.81.refs_5_ = bf16[2,528,128]{2,1,0:T(8,128)(2,1)S(1)} custom-call(s32[1]{0:T(128)} %bitcast.4.at_ref, bf16[1024,256]{1,0:T(8,128)(2,1)} %collective-permute-done.9.refs_0_, bf16[1024,768]{1,0:T(8,128)(2,1)S(1)} %copy-done.1, bf16[1024,768]{1,0:T(8,128)(2,1)} %collective-permute-done.6.refs_2_, bf16[1024,256]{1,0:T(8,128)(2,1)S(1)} %copy-done.7, ...), custom_call_target="tpu_custom_call" | custom-call | flops 11960000512 | bytes 100000 | tf_op jit(solution)/shard_map/pallas_call | solution.py:143
  86.0 6.8 %shard_map.82.refs_0_ = bf16[2,528,128]{2,1,0:T(8,128)(2,1)S(1)} custom-call(s32[1]{0:T(128)} %bitcast.4.at_ref, bf16[1024,256]{1,0:T(8,128)(2,1)} %collective-permute-done.9.refs_0_, bf16[1024,768]{1,0:T(8,128)(2,1)S(1)} %copy-done.1, bf16[1024,768]{1,0:T(8,128)(2,1)} %collective-permute-done.6.refs_2_, bf16[1024,256]{1,0:T(8,128)(2,1)S(1)} %copy-done.5, ...), custom_call_target="tpu_custom_call" | custom-call | flops 11960000512 | bytes 100000 | tf_op jit(solution)/shard_map/pallas_call | solution.py:143
  95.9 6.8 %shard_map.84.a = bf16[2,528,128]{2,1,0:T(8,128)(2,1)S(1)} custom-call(s32[1]{0:T(128)} %bitcast.4.at_ref, bf16[1024,768]{1,0:T(8,128)(2,1)S(1)} %copy-done.1, bf16[1024,768]{1,0:T(8,128)(2,1)S(1)} %copy-done.1, bf16[1024,768]{1,0:T(8,128)(2,1)} %collective-permute-done.6.refs_2_, bf16[1024,256]{1,0:T(8,128)(2,1)S(1)} %copy-done.5, ...), custom_call_target="tpu_custom_call" | custom-call | flops 11960000512 | bytes 100000 | tf_op jit(solution)/shard_map/pallas_call | solution.py:143
  104.7 3.5 %collective-permute-done.13 = bf16[512,128]{1,0:T(8,128)(2,1)S(1)} collective-permute-done((bf16[512,128]{1,0:T(8,128)(2,1)S(1)}, bf16[512,128]{1,0:T(8,128)(2,1)S(1)}, u32[]{:S(2)}, u32[]{:S(2)}) %collective-permute-start.13) | collective-permute-done | bytes 131104 | tf_op jit(solution)/shard_map/ppermute | solution.py:208
  108.2 1.9 %collective-permute-start.16 = (bf16[512,256]{1,0:T(8,128)(2,1)S(1)}, bf16[512,256]{1,0:T(8,128)(2,1)S(1)}, u32[]{:S(2)}, u32[]{:S(2)}) collective-permute-start(bf16[512,256]{1,0:T(8,128)(2,1)S(1)} %constant_dynamic-update-slice_fusion.refs_6_.refs_0_), channel_id=1, source_target_pairs={{0,6},{2,0},{4,2},{6,4},{1,7},{3,1},{5,3},{7,5},{8,14},{10,8},{12,... | collective-permute-start | bytes 786440 | tf_op jit(solution)/shard_map/ppermute | solution.py:222
  110.8 6.9 %shard_map.86.refs_5_ = bf16[2,528,128]{2,1,0:T(8,128)(2,1)S(1)} custom-call(s32[1]{0:T(128)} %bitcast.4.at_ref, bf16[1024,128]{1,0:T(8,128)(2,1)} %collective-permute-done.5.refs_0_, bf16[1024,256]{1,0:T(8,128)(2,1)S(1)} %slice.21.refs_1_, bf16[1024,256]{1,0:T(8,128)(2,1)} %collective-permute-done.refs_2_, ...), custom_call_target="tpu_custom_call" | custom-call | flops 11960000512 | bytes 100000 | tf_op jit(solution)/shard_map/pallas_call | solution.py:143
  118.3 6.8 %shard_map.87.a = bf16[2,528,128]{2,1,0:T(8,128)(2,1)S(1)} custom-call(s32[1]{0:T(128)} %bitcast.4.at_ref, bf16[1024,128]{1,0:T(8,128)(2,1)S(1)} %slice.20.refs_0_, bf16[1024,256]{1,0:T(8,128)(2,1)S(1)} %slice.21.refs_1_, bf16[1024,256]{1,0:T(8,128)(2,1)} %collective-permute-done.refs_2_, bf16[1024,256]{1,0:T(8,128)(2,1)S(1)} %collective-permute-done.3.refs_3_, ...), custom_call_target="tpu_custom_call" | custom-call | flops 11960000512 | bytes 100000 | tf_op jit(solution)/shard_map/pallas_call | solution.py:143
  125.8 5.0 %collective-permute-done.17.refs_2_.refs_3_ = bf16[512,256]{1,0:T(8,128)(2,1)S(1)} collective-permute-done((bf16[512,256]{1,0:T(8,128)(2,1)S(1)}, bf16[512,256]{1,0:T(8,128)(2,1)S(1)}, u32[]{:S(2)}, u32[]{:S(2)}) %collective-permute-start.17) | collective-permute-done | bytes 262176 | tf_op jit(solution)/shard_map/ppermute | solution.py:223
  133.1 2.4 %collective-permute-start.24 = (bf16[512,256]{1,0:T(8,128)(2,1)S(1)}, bf16[512,256]{1,0:T(8,128)(2,1)S(1)}, u32[]{:S(2)}, u32[]{:S(2)}) collective-permute-start(bf16[512,256]{1,0:T(8,128)(2,1)S(1)} %constant_dynamic-update-slice_fusion.2.refs_6_.refs_0_), channel_id=1, source_target_pairs={{0,6},{2,0},{4,2},{6,4},{1,7},{3,1},{5,3},{7,5},{8,14},{10,8},{12,... | collective-permute-start | bytes 786440 | tf_op jit(solution)/shard_map/ppermute | solution.py:222
  135.9 4.0 %collective-permute-done.18 = bf16[512,128]{1,0:T(8,128)(2,1)S(1)} collective-permute-done((bf16[512,128]{1,0:T(8,128)(2,1)S(1)}, bf16[512,128]{1,0:T(8,128)(2,1)S(1)}, u32[]{:S(2)}, u32[]{:S(2)}) %collective-permute-start.18) | collective-permute-done | bytes 131104 | tf_op jit(solution)/shard_map/ppermute | solution.py:208
  140.6 6.5 %collective-permute-done.23.refs_7_.refs_1_ = bf16[512,256]{1,0:T(8,128)(2,1)S(1)} collective-permute-done((bf16[512,256]{1,0:T(8,128)(2,1)S(1)}, bf16[512,256]{1,0:T(8,128)(2,1)S(1)}, u32[]{:S(2)}, u32[]{:S(2)}) %collective-permute-start.23) | collective-permute-done | bytes 262176 | tf_op jit(solution)/shard_map/ppermute | solution.py:221
  147.1 4.6 %shard_map.91.refs_6_ = f32[512,1536]{1,0:T(8,128)S(1)} custom-call(s32[4]{0:T(128)S(1)} %pad_add_fusion.at_ref, bf16[512,256]{1,0:T(8,128)(2,1)S(1)} %constant_dynamic-update-slice_fusion.refs_6_.refs_0_, bf16[512,256]{1,0:T(8,128)(2,1)S(1)} %collective-permute-done.15.refs_0_.refs_1_, bf16[512,256]{1,0:T(8,128)(2,1)S(1)} %collective-permute-done.16.refs_1_.refs_2_, ...), custom_call_target="tpu_custom_call" | custom-call | flops 5520000000 | bytes 100000 | tf_op jit(solution)/shard_map/pallas_call | solution.py:291
  151.7 4.6 %shard_map.92.refs_6_ = f32[512,1536]{1,0:T(8,128)S(1)} custom-call(s32[4]{0:T(128)S(1)} %pad_add_fusion.at_ref, bf16[512,256]{1,0:T(8,128)(2,1)S(1)} %constant_dynamic-update-slice_fusion.2.refs_6_.refs_0_, bf16[512,256]{1,0:T(8,128)(2,1)S(1)} %collective-permute-done.23.refs_7_.refs_1_, bf16[512,256]{1,0:T(8,128)(2,1)S(1)} %collective-permute-done.24.refs_8_.refs_2_, ...), custom_call_target="tpu_custom_call" | custom-call | flops 5520000000 | bytes 100000 | tf_op jit(solution)/shard_map/pallas_call | solution.py:291
  158.1 4.6 %shard_map.93 = (bf16[512,384]{1,0:T(8,128)(2,1)S(1)}, bf16[512,384]{1,0:T(8,128)(2,1)S(1)}, bf16[512,384]{1,0:T(8,128)(2,1)S(1)}, bf16[512,384]{1,0:T(8,128)(2,1)S(1)}) custom-call(s32[4]{0:T(128)S(1)} %pad_add_fusion.at_ref, bf16[512,256]{1,0:T(8,128)(2,1)S(1)} %constant_dynamic-update-slice_fusion.4.refs_6_.refs_0_, ...), custom_call_target="tpu_custom_call" | custom-call | flops 5520000000 | bytes 100000 | tf_op jit(solution)/shard_map/pallas_call | solution.py:291
  164.3 1.8 collective-permute-start.27
  167.4 6.0 %collective-permute-done.26.b = bf16[512,384]{1,0:T(8,128)(2,1)S(1)} collective-permute-done((bf16[512,384]{1,0:T(8,128)(2,1)S(1)}, bf16[512,384]{1,0:T(8,128)(2,1)S(1)}, u32[]{:S(2)}, u32[]{:S(2)}) %collective-permute-start.26) | collective-permute-done | bytes 393248 | tf_op jit(solution)/shard_map/ppermute | solution.py:200
  173.4 10.1 %collective-permute-done.28.d = bf16[512,384]{1,0:T(8,128)(2,1)S(1)} collective-permute-done((bf16[512,384]{1,0:T(8,128)(2,1)S(1)}, bf16[512,384]{1,0:T(8,128)(2,1)S(1)}, u32[]{:S(2)}, u32[]{:S(2)}) %collective-permute-start.28) | collective-permute-done | bytes 393248 | tf_op jit(solution)/shard_map/ppermute | solution.py:200
  (83 shorter events, 24.9 us)
Async XLA Ops:
  3.5 28.8 %all-to-all-start = ((bf16[16,64,768]{2,1,0:T(8,128)(2,1)}), bf16[16,64,768]{2,1,0:T(8,128)(2,1)S(1)}, u32[]{:S(2)}, u32[]{:S(2)}) async-start(bf16[16,64,768]{2,1,0:T(8,128)(2,1)} %shard_map.73.refs_0_.token_ref), calls=%async_computation | async-start | bytes 3145728 | tf_op jit(solution)/shard_map/all_to_all | solution.py:340
  33.6 34.8 %collective-permute-start.6 = (bf16[1024,768]{1,0:T(8,128)(2,1)}, bf16[1024,768]{1,0:T(8,128)(2,1)}, u32[]{:S(2)}, u32[]{:S(2)}) collective-permute-start(bf16[1024,768]{1,0:T(8,128)(2,1)} %shard_map.76.refs_1_.refs_0_), channel_id=1, source_target_pairs={{0,1},{1,0},{2,3},{3,2},{4,5},{5,4},{6,7},{7,6},{8,9},{9,8},{10,11... | collective-permute-start | bytes 4718600 | tf_op jit(solution)/shard_map/ppermute | solution.py:204
  38.6 13.6 %collective-permute-start.1 = (bf16[1024,256]{1,0:T(8,128)(2,1)S(1)}, bf16[1024,256]{1,0:T(8,128)(2,1)S(1)}, u32[]{:S(2)}, u32[]{:S(2)}) collective-permute-start(bf16[1024,256]{1,0:T(8,128)(2,1)S(1)} %get-tuple-element.26), channel_id=1, source_target_pairs={{0,16},{16,0},{32,48},{48,32},{1,17},{17,1},{33,49},{49,33},{2,18}... | collective-permute-start | bytes 1572872 | tf_op jit(solution)/shard_map/ppermute | solution.py:212
  39.8 17.2 %all-to-all-start.1 = ((bf16[16,64,384]{2,1,0:T(8,128)(2,1)}), bf16[16,64,384]{2,1,0:T(8,128)(2,1)S(1)}, u32[]{:S(2)}, u32[]{:S(2)}) async-start(bf16[16,64,384]{2,1,0:T(8,128)(2,1)} %shard_map.77), calls=%async_computation.1 | async-start | bytes 1572864 | tf_op jit(solution)/shard_map/all_to_all | solution.py:340
  53.0 13.0 %collective-permute-start.2 = (bf16[1024,256]{1,0:T(8,128)(2,1)}, bf16[1024,256]{1,0:T(8,128)(2,1)S(1)}, u32[]{:S(2)}, u32[]{:S(2)}) collective-permute-start(bf16[1024,256]{1,0:T(8,128)(2,1)} %shard_map.78), channel_id=1, source_target_pairs={{0,16},{16,0},{32,48},{48,32},{1,17},{17,1},{33,49},{49,33},{2,18}... | collective-permute-start | bytes 1572872 | tf_op jit(solution)/shard_map/ppermute | solution.py:212
  54.2 14.3 %collective-permute-start.8 = (bf16[1024,256]{1,0:T(8,128)(2,1)}, bf16[1024,256]{1,0:T(8,128)(2,1)}, u32[]{:S(2)}, u32[]{:S(2)}) collective-permute-start(bf16[1024,256]{1,0:T(8,128)(2,1)} %copy-done.6), channel_id=1, source_target_pairs={{0,1},{1,0},{2,3},{3,2},{4,5},{5,4},{6,7},{7,6},{8,9},{9,8},{10,11... | collective-permute-start | bytes 1572872 | tf_op jit(solution)/shard_map/ppermute | solution.py:204
  55.2 22.3 %collective-permute-start.9 = (bf16[1024,256]{1,0:T(8,128)(2,1)}, bf16[1024,256]{1,0:T(8,128)(2,1)}, u32[]{:S(2)}, u32[]{:S(2)}) collective-permute-start(bf16[1024,256]{1,0:T(8,128)(2,1)} %get-tuple-element.25), channel_id=1, source_target_pairs={{0,48},{48,0},{16,32},{32,16},{1,49},{49,1},{17,33},{33,17},{2,50}... | collective-permute-start | bytes 1572872 | tf_op jit(solution)/shard_map/ppermute | solution.py:216
  58.0 52.8 %collective-permute-start = (bf16[1024,256]{1,0:T(8,128)(2,1)S(1)}, bf16[1024,256]{1,0:T(8,128)(2,1)}, u32[]{:S(2)}, u32[]{:S(2)}) collective-permute-start(bf16[1024,256]{1,0:T(8,128)(2,1)S(1)} %slice.21.refs_1_), channel_id=1, source_target_pairs={{0,1},{1,0},{2,3},{3,2},{4,5},{5,4},{6,7},{7,6},{8,9},{9,8},{10,11... | collective-permute-start | bytes 1572872 | tf_op jit(solution)/shard_map/ppermute | solution.py:204
  60.0 72.0 %all-to-all-start.2 = ((bf16[4,384,1536]{2,1,0:T(8,128)(2,1)}), bf16[4,384,1536]{2,1,0:T(8,128)(2,1)}, u32[]{:S(2)}, u32[]{:S(2)}) async-start(bf16[4,384,1536]{2,1,0:T(8,128)(2,1)} %shard_map.89), calls=%async_computation.2 | async-start | bytes 9437184 | tf_op jit(solution)/shard_map/all_to_all | solution.py:360
  65.9 44.2 %collective-permute-start.5 = (bf16[1024,128]{1,0:T(8,128)(2,1)S(1)}, bf16[1024,128]{1,0:T(8,128)(2,1)}, u32[]{:S(2)}, u32[]{:S(2)}) collective-permute-start(bf16[1024,128]{1,0:T(8,128)(2,1)S(1)} %slice.20.refs_0_), channel_id=1, source_target_pairs={{0,48},{48,0},{16,32},{32,16},{1,49},{49,1},{17,33},{33,17},{2,50}... | collective-permute-start | bytes 786440 | tf_op jit(solution)/shard_map/ppermute | solution.py:216
  68.4 26.1 %collective-permute-start.3 = (bf16[1024,256]{1,0:T(8,128)(2,1)}, bf16[1024,256]{1,0:T(8,128)(2,1)S(1)}, u32[]{:S(2)}, u32[]{:S(2)}) collective-permute-start(bf16[1024,256]{1,0:T(8,128)(2,1)} %shard_map.79), channel_id=1, source_target_pairs={{0,16},{16,0},{32,48},{48,32},{1,17},{17,1},{33,49},{49,33},{2,18}... | collective-permute-start | bytes 1572872 | tf_op jit(solution)/shard_map/ppermute | solution.py:212
  68.4 17.5 %collective-permute-start.7 = (bf16[1024,256]{1,0:T(8,128)(2,1)}, bf16[1024,256]{1,0:T(8,128)(2,1)S(1)}, u32[]{:S(2)}, u32[]{:S(2)}) collective-permute-start(bf16[1024,256]{1,0:T(8,128)(2,1)} %copy-done.4), channel_id=1, source_target_pairs={{0,1},{1,0},{2,3},{3,2},{4,5},{5,4},{6,7},{7,6},{8,9},{9,8},{10,11... | collective-permute-start | bytes 1572872 | tf_op jit(solution)/shard_map/ppermute | solution.py:204
  84.6 10.5 %collective-permute-start.10 = (bf16[2,528,128]{2,1,0:T(8,128)(2,1)S(1)}, bf16[2,528,128]{2,1,0:T(8,128)(2,1)S(1)}, u32[]{:S(2)}, u32[]{:S(2)}) collective-permute-start(bf16[2,528,128]{2,1,0:T(8,128)(2,1)S(1)} %shard_map.81.refs_5_), channel_id=1, source_target_pairs={{0,48},{48,0},{16,32},{32,16},{1,49},{49,1},{17,33},{33,17},{2,50}... | collective-permute-start | bytes 811016 | tf_op jit(solution)/shard_map/ppermute | solution.py:216
  92.8 9.9 %collective-permute-start.11 = (bf16[2,528,128]{2,1,0:T(8,128)(2,1)S(1)}, bf16[2,528,128]{2,1,0:T(8,128)(2,1)S(1)}, u32[]{:S(2)}, u32[]{:S(2)}) collective-permute-start(bf16[2,528,128]{2,1,0:T(8,128)(2,1)S(1)} %shard_map.82.refs_0_), channel_id=1, source_target_pairs={{0,48},{48,0},{16,32},{32,16},{1,49},{49,1},{17,33},{33,17},{2,50}... | collective-permute-start | bytes 811016 | tf_op jit(solution)/shard_map/ppermute | solution.py:216
  94.5 16.3 %collective-permute-start.4 = (bf16[1024,256]{1,0:T(8,128)(2,1)S(1)}, bf16[1024,256]{1,0:T(8,128)(2,1)S(1)}, u32[]{:S(2)}, u32[]{:S(2)}) collective-permute-start(bf16[1024,256]{1,0:T(8,128)(2,1)S(1)} %collective-permute-done.3.refs_3_), channel_id=1, source_target_pairs={{0,1},{1,0},{2,3},{3,2},{4,5},{5,4},{6,7},{7,6},{8,9},{9,8},{10,11... | collective-permute-start | bytes 1572872 | tf_op jit(solution)/shard_map/ppermute | solution.py:204
  95.5 9.0 %collective-permute-start.12 = (bf16[512,128]{1,0:T(8,128)(2,1)S(1)}, bf16[512,128]{1,0:T(8,128)(2,1)S(1)}, u32[]{:S(2)}, u32[]{:S(2)}) collective-permute-start(bf16[512,128]{1,0:T(8,128)(2,1)S(1)} %get-tuple-element.17), channel_id=1, source_target_pairs={{0,64},{64,0},{1,65},{65,1},{2,66},{66,2},{3,67},{67,3},{4,68},{68... | collective-permute-start | bytes 393224 | tf_op jit(solution)/shard_map/ppermute | solution.py:208
  103.2 5.0 %collective-permute-start.13 = (bf16[512,128]{1,0:T(8,128)(2,1)S(1)}, bf16[512,128]{1,0:T(8,128)(2,1)S(1)}, u32[]{:S(2)}, u32[]{:S(2)}) collective-permute-start(bf16[512,128]{1,0:T(8,128)(2,1)S(1)} %get-tuple-element.18), channel_id=1, source_target_pairs={{0,64},{64,0},{1,65},{65,1},{2,66},{66,2},{3,67},{67,3},{4,68},{68... | collective-permute-start | bytes 393224 | tf_op jit(solution)/shard_map/ppermute | solution.py:208
  104.6 21.3 %collective-permute-start.15 = (bf16[512,256]{1,0:T(8,128)(2,1)S(1)}, bf16[512,256]{1,0:T(8,128)(2,1)S(1)}, u32[]{:S(2)}, u32[]{:S(2)}) collective-permute-start(bf16[512,256]{1,0:T(8,128)(2,1)S(1)} %constant_dynamic-update-slice_fusion.refs_6_.refs_0_), channel_id=1, source_target_pairs={{0,2},{2,4},{4,6},{6,0},{1,3},{3,5},{5,7},{7,1},{8,10},{10,12},{12... | collective-permute-start | bytes 786440 | tf_op jit(solution)/shard_map/ppermute | solution.py:221
  108.2 17.7 %collective-permute-start.16 = (bf16[512,256]{1,0:T(8,128)(2,1)S(1)}, bf16[512,256]{1,0:T(8,128)(2,1)S(1)}, u32[]{:S(2)}, u32[]{:S(2)}) collective-permute-start(bf16[512,256]{1,0:T(8,128)(2,1)S(1)} %constant_dynamic-update-slice_fusion.refs_6_.refs_0_), channel_id=1, source_target_pairs={{0,6},{2,0},{4,2},{6,4},{1,7},{3,1},{5,3},{7,5},{8,14},{10,8},{12,... | collective-permute-start | bytes 786440 | tf_op jit(solution)/shard_map/ppermute | solution.py:222
  110.1 20.7 %collective-permute-start.17 = (bf16[512,256]{1,0:T(8,128)(2,1)S(1)}, bf16[512,256]{1,0:T(8,128)(2,1)S(1)}, u32[]{:S(2)}, u32[]{:S(2)}) collective-permute-start(bf16[512,256]{1,0:T(8,128)(2,1)S(1)} %constant_dynamic-update-slice_fusion.refs_6_.refs_0_), channel_id=1, source_target_pairs={{0,4},{2,6},{4,0},{6,2},{1,5},{3,7},{5,1},{7,3},{8,12},{10,14},{12... | collective-permute-start | bytes 786440 | tf_op jit(solution)/shard_map/ppermute | solution.py:223
  117.6 13.2 %collective-permute-start.14 = (bf16[2,528,128]{2,1,0:T(8,128)(2,1)S(1)}, bf16[2,528,128]{2,1,0:T(8,128)(2,1)S(1)}, u32[]{:S(2)}, u32[]{:S(2)}) collective-permute-start(bf16[2,528,128]{2,1,0:T(8,128)(2,1)S(1)} %shard_map.86.refs_5_), channel_id=1, source_target_pairs={{0,48},{48,0},{16,32},{32,16},{1,49},{49,1},{17,33},{33,17},{2,50}... | collective-permute-start | bytes 811016 | tf_op jit(solution)/shard_map/ppermute | solution.py:216
  131.9 15.2 %collective-permute-start.22 = (bf16[4,384,1536]{2,1,0:T(8,128)(2,1)}, bf16[4,384,1536]{2,1,0:T(8,128)(2,1)}, u32[]{:S(2)}, u32[]{:S(2)}) collective-permute-start(bf16[4,384,1536]{2,1,0:T(8,128)(2,1)} %shard_map.90.refs_4_), channel_id=1, source_target_pairs={{0,1},{1,0},{2,3},{3,2},{4,5},{5,4},{6,7},{7,6},{8,9},{9,8},{10,11... | collective-permute-start | bytes 14155784 | tf_op jit(solution)/shard_map/ppermute | solution.py:204
  132.8 14.3 %collective-permute-start.23 = (bf16[512,256]{1,0:T(8,128)(2,1)S(1)}, bf16[512,256]{1,0:T(8,128)(2,1)S(1)}, u32[]{:S(2)}, u32[]{:S(2)}) collective-permute-start(bf16[512,256]{1,0:T(8,128)(2,1)S(1)} %constant_dynamic-update-slice_fusion.2.refs_6_.refs_0_), channel_id=1, source_target_pairs={{0,2},{2,4},{4,6},{6,0},{1,3},{3,5},{5,7},{7,1},{8,10},{10,12},{12... | collective-permute-start | bytes 786440 | tf_op jit(solution)/shard_map/ppermute | solution.py:221
  133.1 14.0 %collective-permute-start.24 = (bf16[512,256]{1,0:T(8,128)(2,1)S(1)}, bf16[512,256]{1,0:T(8,128)(2,1)S(1)}, u32[]{:S(2)}, u32[]{:S(2)}) collective-permute-start(bf16[512,256]{1,0:T(8,128)(2,1)S(1)} %constant_dynamic-update-slice_fusion.2.refs_6_.refs_0_), channel_id=1, source_target_pairs={{0,6},{2,0},{4,2},{6,4},{1,7},{3,1},{5,3},{7,5},{8,14},{10,8},{12,... | collective-permute-start | bytes 786440 | tf_op jit(solution)/shard_map/ppermute | solution.py:222
  135.5 11.6 %collective-permute-start.25 = (bf16[512,256]{1,0:T(8,128)(2,1)S(1)}, bf16[512,256]{1,0:T(8,128)(2,1)S(1)}, u32[]{:S(2)}, u32[]{:S(2)}) collective-permute-start(bf16[512,256]{1,0:T(8,128)(2,1)S(1)} %constant_dynamic-update-slice_fusion.2.refs_6_.refs_0_), channel_id=1, source_target_pairs={{0,4},{2,6},{4,0},{6,2},{1,5},{3,7},{5,1},{7,3},{8,12},{10,14},{12... | collective-permute-start | bytes 786440 | tf_op jit(solution)/shard_map/ppermute | solution.py:223
  135.5 4.4 %collective-permute-start.18 = (bf16[512,128]{1,0:T(8,128)(2,1)S(1)}, bf16[512,128]{1,0:T(8,128)(2,1)S(1)}, u32[]{:S(2)}, u32[]{:S(2)}) collective-permute-start(bf16[512,128]{1,0:T(8,128)(2,1)S(1)} %get-tuple-element.20), channel_id=1, source_target_pairs={{0,64},{64,0},{1,65},{65,1},{2,66},{66,2},{3,67},{67,3},{4,68},{68... | collective-permute-start | bytes 393224 | tf_op jit(solution)/shard_map/ppermute | solution.py:208
  139.9 16.4 %collective-permute-start.19 = (bf16[512,256]{1,0:T(8,128)(2,1)S(1)}, bf16[512,256]{1,0:T(8,128)(2,1)S(1)}, u32[]{:S(2)}, u32[]{:S(2)}) collective-permute-start(bf16[512,256]{1,0:T(8,128)(2,1)S(1)} %constant_dynamic-update-slice_fusion.4.refs_6_.refs_0_), channel_id=1, source_target_pairs={{0,2},{2,4},{4,6},{6,0},{1,3},{3,5},{5,7},{7,1},{8,10},{10,12},{12... | collective-permute-start | bytes 786440 | tf_op jit(solution)/shard_map/ppermute | solution.py:221
  147.1 9.3 %collective-permute-start.20 = (bf16[512,256]{1,0:T(8,128)(2,1)S(1)}, bf16[512,256]{1,0:T(8,128)(2,1)S(1)}, u32[]{:S(2)}, u32[]{:S(2)}) collective-permute-start(bf16[512,256]{1,0:T(8,128)(2,1)S(1)} %constant_dynamic-update-slice_fusion.4.refs_6_.refs_0_), channel_id=1, source_target_pairs={{0,6},{2,0},{4,2},{6,4},{1,7},{3,1},{5,3},{7,5},{8,14},{10,8},{12,... | collective-permute-start | bytes 786440 | tf_op jit(solution)/shard_map/ppermute | solution.py:222
  147.1 11.0 %collective-permute-start.21 = (bf16[512,256]{1,0:T(8,128)(2,1)S(1)}, bf16[512,256]{1,0:T(8,128)(2,1)S(1)}, u32[]{:S(2)}, u32[]{:S(2)}) collective-permute-start(bf16[512,256]{1,0:T(8,128)(2,1)S(1)} %constant_dynamic-update-slice_fusion.4.refs_6_.refs_0_), channel_id=1, source_target_pairs={{0,4},{2,6},{4,0},{6,2},{1,5},{3,7},{5,1},{7,3},{8,12},{10,14},{12... | collective-permute-start | bytes 786440 | tf_op jit(solution)/shard_map/ppermute | solution.py:223
  162.7 10.7 %collective-permute-start.26 = (bf16[512,384]{1,0:T(8,128)(2,1)S(1)}, bf16[512,384]{1,0:T(8,128)(2,1)S(1)}, u32[]{:S(2)}, u32[]{:S(2)}) collective-permute-start(bf16[512,384]{1,0:T(8,128)(2,1)S(1)} %get-tuple-element.22), channel_id=1, source_target_pairs={{0,8},{1,9},{8,0},{9,1},{2,10},{3,11},{10,2},{11,3},{4,12},{5,13},... | collective-permute-start | bytes 1179656 | tf_op jit(solution)/shard_map/ppermute | solution.py:200
  164.3 9.1 %collective-permute-start.27 = (bf16[512,384]{1,0:T(8,128)(2,1)S(1)}, bf16[512,384]{1,0:T(8,128)(2,1)S(1)}, u32[]{:S(2)}, u32[]{:S(2)}) collective-permute-start(bf16[512,384]{1,0:T(8,128)(2,1)S(1)} %get-tuple-element.23), channel_id=1, source_target_pairs={{0,1},{1,0},{2,3},{3,2},{4,5},{5,4},{6,7},{7,6},{8,9},{9,8},{10,11... | collective-permute-start | bytes 1179656 | tf_op jit(solution)/shard_map/ppermute | solution.py:204
  166.1 17.5 %collective-permute-start.28 = (bf16[512,384]{1,0:T(8,128)(2,1)S(1)}, bf16[512,384]{1,0:T(8,128)(2,1)S(1)}, u32[]{:S(2)}, u32[]{:S(2)}) collective-permute-start(bf16[512,384]{1,0:T(8,128)(2,1)S(1)} %get-tuple-element.24), channel_id=1, source_target_pairs={{0,9},{1,8},{8,1},{9,0},{2,11},{3,10},{10,3},{11,2},{4,13},{5,12},... | collective-permute-start | bytes 1179656 | tf_op jit(solution)/shard_map/ppermute | solution.py:200
  (9 other events, 41.6 us)
